TPU v7x, 512 devices: a whole 4x8x8 slice. The times are simulated.
512 devices in a mesh: dp: 16 (over y, core), ctx: 32 (over z, x).
Axes of the slice: x: 4, y: 8, z: 8, core: 2. Of those that a mesh axis runs over, the one named last changes fastest.
Arguments:
- queries: bfloat16 [16, 4096, 1536], P('dp', 'ctx'), may hold values from -6 to 6
- keys: bfloat16 [16, 4096, 1536], P('dp', 'ctx'), may hold values from -6 to 6
- values: bfloat16 [16, 4096, 1536], P('dp', 'ctx'), may hold values from -6 to 6
- out_grad: bfloat16 [16, 4096, 1536], P('dp', 'ctx'), may hold values from -54 to 54
- norm_gains: float32 [2, 128], replicated, may hold values from 0.5 to 8
- tile_image: int32 [16, 16], P('dp'), may hold values from 0 to 11, never falling along the last dimension, each value on 1 to 2 neighbouring positions
Outputs:
- query_grad: bfloat16 [16, 4096, 1536], P('dp', 'ctx')
- key_grad: bfloat16 [16, 4096, 1536], P('dp', 'ctx')
- value_grad: bfloat16 [16, 4096, 1536], P('dp', 'ctx')
- gain_grad: float32 [2, 128], replicated
Inputs may be any that keep to these rules, and one draw needn't show every extreme that they name: `tile_image`: each tile is 256 consecutive positions of the replica's packed sequence.
All inputs are finite; a program needn't handle non-finite values.
Results may differ from a plain program's by a relative error of at most 0.0075.
The roundings to bfloat16 on the way count: a program that leaves them out, or rounds other values in their place, can miss the bound.
Values may be sent and summed in bfloat16 or wider, within the bound.
No kernel may reach another device: no remote copies, remote signals or barrier semaphores. Data moves between devices by JAX's collectives and lax.ppermute only.
A program may use at most 64 MiB of HBM per device.

v0:
```python
import math

import jax
import jax.numpy as jnp
from jax import lax
from jax.sharding import PartitionSpec as P

epsilon = 1e-06


def for_sending(x):
    return jax.tree.map(lambda a: a.astype(jnp.bfloat16) if a.dtype == jnp.float32 else a, x)


def normalize(token_rows, gain):
    row_count = token_rows.shape[0]
    raw_values = token_rows.astype(jnp.float32).reshape(row_count, -1, gain.shape[0])
    inverse = lax.rsqrt(jnp.mean(raw_values * raw_values, axis=-1, keepdims=True) + epsilon)
    unit_rows = raw_values * inverse
    return (unit_rows, inverse, (unit_rows * gain).astype(jnp.bfloat16).reshape(row_count, -1))


def norm_back(grad_norm, unit_rows, inverse, gain):
    grad_values = grad_norm.astype(jnp.float32).reshape(unit_rows.shape)
    direct = grad_values * gain
    inner_term = jnp.mean(direct * unit_rows, axis=-1, keepdims=True)
    result = inverse * (direct - unit_rows * inner_term)
    return (
        result.reshape(unit_rows.shape[0], -1).astype(jnp.bfloat16),
        jnp.sum(grad_values * unit_rows, axis=(0, 1)),
    )


def head_grads(query_rows, key_rows, value_rows, grad_rows):
    score_scale = 1.0 / math.sqrt(query_rows.shape[-1])
    scores = (
        jnp.einsum("qd,kd->qk", query_rows, key_rows, preferred_element_type=jnp.float32)
        * score_scale
    )
    row_top = jnp.max(scores, axis=-1, keepdims=True)
    log_total = row_top + jnp.log(jnp.sum(jnp.exp(scores - row_top), axis=-1, keepdims=True))
    weights = jnp.exp(scores - log_total)
    weight_grad = jnp.einsum("qd,kd->qk", grad_rows, value_rows, preferred_element_type=jnp.float32)
    row_inner = jnp.sum(weights * weight_grad, axis=-1, keepdims=True)
    score_grad = (weights * (weight_grad - row_inner)).astype(jnp.bfloat16)
    value_grad = jnp.einsum(
        "qk,qd->kd", weights.astype(jnp.bfloat16), grad_rows, preferred_element_type=jnp.float32
    )
    query_grad = (
        jnp.einsum("qk,kd->qd", score_grad, key_rows, preferred_element_type=jnp.float32)
        * score_scale
    )
    key_grad = (
        jnp.einsum("qk,qd->kd", score_grad, query_rows, preferred_element_type=jnp.float32)
        * score_scale
    )
    return (
        query_grad.astype(jnp.bfloat16),
        key_grad.astype(jnp.bfloat16),
        value_grad.astype(jnp.bfloat16),
    )


def one_head(pieces):
    return jax.vmap(head_grads)(pieces[0], pieces[1], pieces[2], pieces[3])


def attend(stacked):
    heads_first = tuple((jnp.moveaxis(member, 2, 0) for member in stacked))
    results = lax.map(one_head, heads_first)
    return tuple((jnp.moveaxis(result, 0, 2) for result in results))


def paired(blocks):
    block_shape = blocks[0].shape
    reshaped = tuple(
        (
            member.reshape(
                block_shape[0],
                block_shape[1] * block_shape[2],
                block_shape[3] * block_shape[4],
                block_shape[5],
            )
            for member in blocks
        )
    )
    return tuple((result.reshape(block_shape) for result in attend(reshaped)))


def whole_image(blocks):
    block_shape = blocks[0].shape
    reshaped = tuple(
        (
            member.reshape(
                1,
                block_shape[0] * block_shape[1] * block_shape[2],
                block_shape[3] * block_shape[4],
                block_shape[5],
            )
            for member in blocks
        )
    )
    return tuple((result.reshape(block_shape) for result in attend(reshaped)))


def owner_plan(images, shards):
    tile_count = images.shape[0]
    tile_ids = jnp.arange(tile_count, dtype=jnp.int32)
    filler = jnp.full((1,), -1, jnp.int32)
    earlier = jnp.concatenate([filler, images[:-1]])
    following = jnp.concatenate([images[1:], filler])
    starts = images != earlier
    longer = starts & (following == images)
    shorter = starts & (following != images)
    long_rank = jnp.cumsum(longer.astype(jnp.int32)) - 1
    short_rank = jnp.cumsum(shorter.astype(jnp.int32)) - 1
    long_count = jnp.sum(longer.astype(jnp.int32))
    in_long = jnp.logical_not(shorter)
    tile_owner = jnp.where(in_long, long_rank, long_count + short_rank // 2)
    tile_slot = jnp.where(in_long, jnp.where(starts, 0, 1), short_rank % 2)
    owners = jnp.arange(shards, dtype=jnp.int32)
    slot_ids = jnp.arange(2, dtype=jnp.int32)
    matches = (tile_owner[None, None, :] == owners[:, None, None]) & (
        tile_slot[None, None, :] == slot_ids[None, :, None]
    )
    slot_tile = jnp.sum(jnp.where(matches, tile_ids, 0), axis=-1)
    slot_valid = jnp.any(matches, axis=-1)
    return (slot_tile, slot_valid, long_count)


def pack_rows(token_rows, slot_index, slot_live, tile_count, head_dim, part_count):
    per_tile = token_rows.shape[0] // tile_count
    item_count = token_rows.shape[1] // (part_count * head_dim)
    blocks = token_rows.reshape(tile_count, per_tile, part_count, item_count, head_dim).transpose(
        0, 2, 1, 3, 4
    )
    blocks = blocks.reshape(tile_count * part_count, per_tile, item_count, head_dim)
    picked = jnp.take(blocks, slot_index.reshape(-1), axis=0).reshape(
        slot_index.shape + (per_tile, item_count, head_dim)
    )
    picked = jnp.where(
        slot_live[:, :, :, None, None, None], picked, jnp.zeros((), token_rows.dtype)
    )
    return picked.transpose(1, 3, 0, 4, 2, 5)


def unpack_rows(incoming, slot_index, slot_live, tile_count, part_count):
    per_tile = incoming.shape[1]
    shards = incoming.shape[2]
    item_count = incoming.shape[3]
    head_dim = incoming.shape[5]
    reshaped = incoming.transpose(2, 0, 4, 1, 3, 5).reshape(
        shards * incoming.shape[0] * incoming.shape[4], per_tile, item_count, head_dim
    )
    target = jnp.where(slot_live, slot_index, part_count * tile_count).reshape(-1)
    placed = (
        jnp.zeros((part_count * tile_count, per_tile, item_count, head_dim), incoming.dtype)
        .at[target]
        .set(reshaped, mode="drop")
    )
    placed = placed.reshape(tile_count, part_count, per_tile, item_count, head_dim).transpose(
        0, 2, 1, 3, 4
    )
    return placed.reshape(tile_count * per_tile, part_count * item_count * head_dim)


def on_device(queries, keys, values, out_grad, norm_gains, tile_image):
    shards = lax.axis_size("ctx")
    own_index = lax.axis_index("ctx")
    head_dim = norm_gains.shape[1]
    tile_count = tile_image.shape[1]
    query_unit, query_inverse, query_norm = normalize(queries[0], norm_gains[0])
    key_unit, key_inverse, key_norm = normalize(keys[0], norm_gains[1])
    slot_tile, slot_valid, long_count = owner_plan(tile_image[0], shards)
    owners = jnp.arange(shards, dtype=jnp.int32)
    lower_half = slot_tile * 2
    whole_owner = owners < long_count
    part_count = 2
    slot_index = jnp.stack([lower_half, lower_half + 1], axis=-1)
    slot_live = jnp.stack([slot_valid, slot_valid], axis=-1)
    own_flag = whole_owner[own_index]
    outgoing = tuple(
        (
            pack_rows(token_rows, slot_index, slot_live, tile_count, head_dim, part_count)
            for token_rows in (query_norm, key_norm, values[0], out_grad[0])
        )
    )
    outputs = lax.cond(
        own_flag,
        whole_image,
        paired,
        (
            lax.all_to_all(outgoing[0], "ctx", split_axis=2, concat_axis=2, tiled=True),
            lax.all_to_all(outgoing[1], "ctx", split_axis=2, concat_axis=2, tiled=True),
            lax.all_to_all(outgoing[2], "ctx", split_axis=2, concat_axis=2, tiled=True),
            lax.all_to_all(outgoing[3], "ctx", split_axis=2, concat_axis=2, tiled=True),
        ),
    )
    returned = jax.tree.map(
        lambda part, own: part.astype(own.dtype),
        lax.all_to_all(for_sending(outputs), "ctx", split_axis=2, concat_axis=2, tiled=True),
        outputs,
    )
    query_norm_grad = unpack_rows(returned[0], slot_index, slot_live, tile_count, part_count)
    key_norm_grad = unpack_rows(returned[1], slot_index, slot_live, tile_count, part_count)
    value_grad = unpack_rows(returned[2], slot_index, slot_live, tile_count, part_count)
    query_grad, query_term = norm_back(query_norm_grad, query_unit, query_inverse, norm_gains[0])
    key_grad, key_term = norm_back(key_norm_grad, key_unit, key_inverse, norm_gains[1])
    gain_grad = lax.psum(jnp.stack([query_term, key_term]), ("dp", "ctx"))
    return (query_grad[None], key_grad[None], value_grad[None], gain_grad)


def solution(mesh):
    in_specs = (
        P("dp", "ctx", None),
        P("dp", "ctx", None),
        P("dp", "ctx", None),
        P("dp", "ctx", None),
        P(),
        P("dp", None),
    )
    out_specs = (P("dp", "ctx", None), P("dp", "ctx", None), P("dp", "ctx", None), P())
    return jax.shard_map(
        on_device, mesh=mesh, in_specs=in_specs, out_specs=out_specs, check_vma=False
    )
```

profile of v0, /device:TPU:1, one launch (start us, length us, event | category | flops | bytes accessed | tf_op | source)
XLA Modules:
  0.0 544.1 jit_solution(17885836436405776744)
XLA Ops:
  2.5 1.3 fusion.73
  3.9 1.3 add_select_fusion
  5.4 1.2 copy.128
  10.5 1.3 multiply_convert_fusion.3
  12.6 1.9 gather_fusion.1
  14.5 1.9 gather_fusion.2
  16.4 1.9 gather_fusion.3
  18.5 2.8 broadcast_select_fusion
  21.3 1.5 select_bitcast_fusion
  22.8 52.0 %all_to_all.35 = bf16[2,8,32,6,2,128]{5,1,3,4,0,2:T(8,128)(2,1)S(1)} all-to-all(bf16[2,8,32,6,2,128]{5,1,3,4,0,2:T(8,128)(2,1)S(1)} %get-tuple-element.232), channel_id=1, replica_groups=mesh['dp'=16,'ctx'=32] {'ctx'}, dimensions={2} | all-to-all | bytes 3145728 | tf_op jit(solution)/shard_map/all_to_all | solution.py:193
  74.8 42.8 %all_to_all.36 = bf16[2,8,32,6,2,128]{5,1,3,4,0,2:T(8,128)(2,1)S(1)} all-to-all(bf16[2,8,32,6,2,128]{5,1,3,4,0,2:T(8,128)(2,1)S(1)} %get-tuple-element.230), channel_id=1, replica_groups=mesh['dp'=16,'ctx'=32] {'ctx'}, dimensions={2} | all-to-all | bytes 3145728 | tf_op jit(solution)/shard_map/all_to_all | solution.py:194
  117.6 43.4 %all_to_all.37 = bf16[2,8,32,6,2,128]{5,1,3,4,0,2:T(8,128)(2,1)} all-to-all(bf16[2,8,32,6,2,128]{5,1,3,4,0,2:T(8,128)(2,1)S(1)} %get-tuple-element.231), channel_id=1, replica_groups=mesh['dp'=16,'ctx'=32] {'ctx'}, dimensions={2} | all-to-all | bytes 3145728 | tf_op jit(solution)/shard_map/all_to_all | solution.py:195
  161.1 6.3 %all-to-all-start.3 = ((bf16[2,8,32,6,2,128]{5,1,3,4,0,2:T(8,128)(2,1)}), bf16[2,8,32,6,2,128]{5,1,3,4,0,2:T(8,128)(2,1)}, u32[]{:S(2)}, u32[]{:S(2)}) async-start(bf16[2,8,32,6,2,128]{5,1,3,4,0,2:T(8,128)(2,1)} %get-tuple-element.229), calls=%async_computation.3 | async-start | bytes 3145728 | tf_op jit(solution)/shard_map/all_to_all | solution.py:196
  169.2 33.9 %all-to-all-done.3 = bf16[2,8,32,6,2,128]{5,1,3,4,0,2:T(8,128)(2,1)} async-done(((bf16[2,8,32,6,2,128]{5,1,3,4,0,2:T(8,128)(2,1)}), bf16[2,8,32,6,2,128]{5,1,3,4,0,2:T(8,128)(2,1)}, u32[]{:S(2)}, u32[]{:S(2)}) %all-to-all-start.3) | async-done | bytes 1572896 | tf_op jit(solution)/shard_map/all_to_all | solution.py:196
  203.1 88.8 %conditional.1 = (bf16[2,8,32,6,2,128]{5,2,1,0,4,3:T(8,128)(2,1)}, bf16[2,8,32,6,2,128]{5,2,1,0,4,3:T(8,128)(2,1)}, bf16[2,8,32,6,2,128]{5,2,1,0,4,3:T(8,128)(2,1)}) conditional(s32[]{:T(128)} %bitcast.53, (bf16[2,8,32,6,2,128]{5,1,3,4,0,2:T(8,128)(2,1)S(1)}, bf16[2,8,32,6,2,128]{5,1,3,4,0,2:T(8,128)(2,1)S(1)}, ...), branch_computations={%region_7.14_spmd, %region_13.20_spmd} | conditional | flops 339278848 | bytes 29125856 | solution.py:188
  203.1 2.2 copy.142
  206.2 2.5 copy.145
  208.8 2.2 copy.144
  211.0 80.9 %while.27 = (s32[]{:T(128)}, bf16[12,1,512,128]{3,2,1,0:T(8,128)(2,1)}, bf16[12,1,512,128]{3,2,1,0:T(8,128)(2,1)}, bf16[12,1,512,128]{3,2,1,0:T(8,128)(2,1)}, bf...) while((s32[]{:T(128)}, ...), condition=%wide.region_18.19_spmd, body=%wide.region_14.18_spmd.sunk | while | flops 339278848 | bytes 10251357 | solution.py:70
  212.4 1.2 multiply_reduce_fusion.4
  213.9 1.9 fusion.109
  217.7 1.2 fusion.107
  219.1 1.2 multiply_reduce_fusion.4
  220.7 1.9 fusion.109
  225.9 1.2 multiply_reduce_fusion.4
  227.4 1.8 fusion.109
  232.6 1.2 multiply_reduce_fusion.4
  234.1 1.9 fusion.109
  239.3 1.2 multiply_reduce_fusion.4
  240.8 1.8 fusion.109
  246.1 1.2 multiply_reduce_fusion.4
  247.6 1.9 fusion.109
  251.4 1.2 fusion.107
  252.8 1.2 multiply_reduce_fusion.4
  254.3 1.9 fusion.109
  258.1 1.2 fusion.107
  259.6 1.2 multiply_reduce_fusion.4
  261.1 1.9 fusion.109
  266.3 1.2 multiply_reduce_fusion.4
  267.8 1.9 fusion.109
  273.0 1.2 multiply_reduce_fusion.4
  274.5 1.9 fusion.109
  278.3 1.2 fusion.107
  279.8 1.2 multiply_reduce_fusion.4
  281.3 1.9 fusion.109
  285.1 1.2 fusion.107
  286.5 1.2 multiply_reduce_fusion.4
  288.0 1.9 fusion.109
  291.9 3.2 copy.150
  295.0 12.4 %all-to-all-start.5 = ((bf16[2,8,32,6,2,128]{5,1,3,4,0,2:T(8,128)(2,1)}), bf16[2,8,32,6,2,128]{5,1,3,4,0,2:T(8,128)(2,1)S(1)}, u32[]{:S(2)}, u32[]{:S(2)}) async-start(bf16[2,8,32,6,2,128]{5,1,3,4,0,2:T(8,128)(2,1)} %copy.150), calls=%async_computation.5 | async-start | bytes 3145728 | tf_op jit(solution)/shard_map/all_to_all | solution.py:201
  307.5 3.2 copy.146
  310.6 32.1 %all-to-all-done.5 = bf16[2,8,32,6,2,128]{5,1,3,4,0,2:T(8,128)(2,1)S(1)} async-done(((bf16[2,8,32,6,2,128]{5,1,3,4,0,2:T(8,128)(2,1)}), bf16[2,8,32,6,2,128]{5,1,3,4,0,2:T(8,128)(2,1)S(1)}, u32[]{:S(2)}, u32[]{:S(2)}) %all-to-all-start.5) | async-done | bytes 1572896 | tf_op jit(solution)/shard_map/all_to_all | solution.py:201
  343.8 7.7 %all-to-all-start.4 = ((bf16[2,8,32,6,2,128]{5,1,3,4,0,2:T(8,128)(2,1)}), bf16[2,8,32,6,2,128]{5,1,3,4,0,2:T(8,128)(2,1)S(1)}, u32[]{:S(2)}, u32[]{:S(2)}) async-start(bf16[2,8,32,6,2,128]{5,1,3,4,0,2:T(8,128)(2,1)} %copy.146), calls=%async_computation.4 | async-start | bytes 3145728 | tf_op jit(solution)/shard_map/all_to_all | solution.py:201
  351.5 3.2 copy.156
  354.7 32.0 %all-to-all-done.4 = bf16[2,8,32,6,2,128]{5,1,3,4,0,2:T(8,128)(2,1)S(1)} async-done(((bf16[2,8,32,6,2,128]{5,1,3,4,0,2:T(8,128)(2,1)}), bf16[2,8,32,6,2,128]{5,1,3,4,0,2:T(8,128)(2,1)S(1)}, u32[]{:S(2)}, u32[]{:S(2)}) %all-to-all-start.4) | async-done | bytes 1572896 | tf_op jit(solution)/shard_map/all_to_all | solution.py:201
  386.7 8.0 %all-to-all-start.6 = ((bf16[2,8,32,6,2,128]{5,1,3,4,0,2:T(8,128)(2,1)}), bf16[2,8,32,6,2,128]{5,1,3,4,0,2:T(8,128)(2,1)S(1)}, u32[]{:S(2)}, u32[]{:S(2)}) async-start(bf16[2,8,32,6,2,128]{5,1,3,4,0,2:T(8,128)(2,1)} %copy.156), calls=%async_computation.6 | async-start | bytes 3145728 | tf_op jit(solution)/shard_map/all_to_all | solution.py:201
  396.0 2.3 copy.155
  399.5 12.0 %scatter_fusion.1 = bf16[32,8,6,128]{3,1,2,0:T(8,128)(2,1)S(1)} fusion(bf16[32,8,6,128]{3,1,2,0:T(8,128)(2,1)S(1)} %broadcast.323.clone.1, s32[128]{0:T(128)} %fusion.74, bf16[128,8,6,128]{3,1,2,0:T(8,128)(2,1)} %bitcast.329), kind=kCustom, calls=%fused_computation.5 | custom fusion | bytes 4719104 | tf_op jit(solution)/shard_map/scatter | solution.py:159
  411.5 2.3 fusion.65
  415.5 11.9 %scatter_fusion = bf16[32,8,6,128]{3,1,2,0:T(8,128)(2,1)S(1)} fusion(bf16[32,8,6,128]{3,1,2,0:T(8,128)(2,1)S(1)} %broadcast.323.clone, s32[128]{0:T(128)S(1)} %copy-done.25, bf16[128,8,6,128]{3,1,2,0:T(8,128)(2,1)} %bitcast.328), kind=kCustom, calls=%fused_computation.4 | custom fusion | bytes 4719104 | tf_op jit(solution)/shard_map/scatter | solution.py:159
  430.1 1.4 copy.147
  434.1 100.2 %psum.7 = f32[2,128]{1,0:T(2,128)} all-reduce(f32[2,128]{1,0:T(2,128)S(1)} %pad_maximum_fusion), channel_id=1, replica_groups=mesh['dp'=16,'ctx'=32] {'dp','ctx'}, use_global_device_ids=true, to_apply=%region_26.28 | all-reduce | flops 256 | bytes 2048 | tf_op jit(solution)/shard_map/psum | solution.py:209
  535.4 6.1 %scatter_fusion.2 = bf16[32,8,6,128]{3,1,2,0:T(8,128)(2,1)S(1)} fusion(bf16[32,8,6,128]{3,1,2,0:T(8,128)(2,1)S(1)} %broadcast.323.clone.2, s32[128]{0:T(128)S(1)} %copy-done.26, bf16[128,8,6,128]{3,1,2,0:T(8,128)(2,1)S(1)} %bitcast.327), kind=kCustom, calls=%fused_computation.6 | custom fusion | bytes 4719104 | tf_op jit(solution)/shard_map/scatter | solution.py:159
  541.5 2.5 multiply_convert_fusion.2
  (192 shorter events, 58.0 us)
Async XLA Ops:
  0.6 13.9 %copy-start = (bf16[1,128,1536]{2,1,0:T(8,128)(2,1)S(1)}, bf16[1,128,1536]{2,1,0:T(8,128)(2,1)}, u32[]{:S(2)}) copy-start(bf16[1,128,1536]{2,1,0:T(8,128)(2,1)} %param.16) | copy-start | bytes 1179652
  6.7 2.9 copy-start.10
  6.7 3.1 copy-start.28
  6.7 3.1 copy-start.12
  7.0 3.5 copy-start.8
  9.8 0.7 copy-start.15
  9.8 0.6 copy-start.20
  9.8 0.6 copy-start.23
  10.4 1.4 copy-start.18
  10.4 1.3 copy-start.17
  14.5 1.9 copy-start.5
  16.4 1.9 copy-start.27
  16.4 2.0 copy-start.29
  161.1 42.0 %all-to-all-start.3 = ((bf16[2,8,32,6,2,128]{5,1,3,4,0,2:T(8,128)(2,1)}), bf16[2,8,32,6,2,128]{5,1,3,4,0,2:T(8,128)(2,1)}, u32[]{:S(2)}, u32[]{:S(2)}) async-start(bf16[2,8,32,6,2,128]{5,1,3,4,0,2:T(8,128)(2,1)} %get-tuple-element.229), calls=%async_computation.3 | async-start | bytes 3145728 | tf_op jit(solution)/shard_map/all_to_all | solution.py:196
  206.2 2.6 copy-start.4
  295.0 47.7 %all-to-all-start.5 = ((bf16[2,8,32,6,2,128]{5,1,3,4,0,2:T(8,128)(2,1)}), bf16[2,8,32,6,2,128]{5,1,3,4,0,2:T(8,128)(2,1)S(1)}, u32[]{:S(2)}, u32[]{:S(2)}) async-start(bf16[2,8,32,6,2,128]{5,1,3,4,0,2:T(8,128)(2,1)} %copy.150), calls=%async_computation.5 | async-start | bytes 3145728 | tf_op jit(solution)/shard_map/all_to_all | solution.py:201
  342.7 1.1 copy-start.7
  343.8 42.9 %all-to-all-start.4 = ((bf16[2,8,32,6,2,128]{5,1,3,4,0,2:T(8,128)(2,1)}), bf16[2,8,32,6,2,128]{5,1,3,4,0,2:T(8,128)(2,1)S(1)}, u32[]{:S(2)}, u32[]{:S(2)}) async-start(bf16[2,8,32,6,2,128]{5,1,3,4,0,2:T(8,128)(2,1)} %copy.146), calls=%async_computation.4 | async-start | bytes 3145728 | tf_op jit(solution)/shard_map/all_to_all | solution.py:201
  354.7 40.0 %copy-start.19 = (s32[32,2,2]{0,1,2:T(2,128)S(1)}, s32[32,2,2]{0,1,2:T(2,128)}, u32[]{:S(2)}) copy-start(s32[32,2,2]{0,1,2:T(2,128)} %get-tuple-element.234) | copy-start | bytes 1540
  386.7 24.8 %copy-start.6 = (bf16[2,8,32,6,2,128]{5,1,3,4,0,2:T(8,128)(2,1)}, bf16[2,8,32,6,2,128]{5,1,3,4,0,2:T(8,128)(2,1)S(1)}, u32[]{:S(2)}) copy-start(bf16[2,8,32,6,2,128]{5,1,3,4,0,2:T(8,128)(2,1)S(1)} %all-to-all-done.4) | copy-start | bytes 4718596
  386.7 148.6 %all-to-all-start.6 = ((bf16[2,8,32,6,2,128]{5,1,3,4,0,2:T(8,128)(2,1)}), bf16[2,8,32,6,2,128]{5,1,3,4,0,2:T(8,128)(2,1)S(1)}, u32[]{:S(2)}, u32[]{:S(2)}) async-start(bf16[2,8,32,6,2,128]{5,1,3,4,0,2:T(8,128)(2,1)} %copy.156), calls=%async_computation.6 | async-start | bytes 3145728 | tf_op jit(solution)/shard_map/all_to_all | solution.py:201
  394.7 4.1 copy-start.24
  394.7 4.1 copy-start.21
  413.9 1.5 copy-start.25
  415.4 12.0 %copy-start.9 = (f32[1,128,1536]{2,1,0:T(8,128)S(1)}, f32[1,128,1536]{2,1,0:T(8,128)}, u32[]{:S(2)}) copy-start(f32[1,128,1536]{2,1,0:T(8,128)} %copy-done.8) | copy-start | bytes 2359300
  415.4 12.0 %copy-start.16 = (f32[16,8,2,6]{1,3,2,0:T(8,128)S(1)}, f32[16,8,2,6]{1,3,2,0:T(8,128)}, u32[]{:S(2)}) copy-start(f32[16,8,2,6]{1,3,2,0:T(8,128)} %copy-done.15) | copy-start | bytes 18436
  415.5 12.0 %copy-start.22 = (f32[128]{0:T(128)S(1)}, f32[128]{0:T(128)}, u32[]{:S(2)}) copy-start(f32[128]{0:T(128)} %copy-done.20) | copy-start | bytes 1540
  428.3 3.2 copy-start.11
  432.5 102.8 %copy-start.26 = (s32[128]{0:T(128)S(1)}, s32[128]{0:T(128)}, u32[]{:S(2)}) copy-start(s32[128]{0:T(128)} %fusion.74) | copy-start | bytes 1540
  535.3 6.2 %copy-start.13 = (bf16[1,128,1536]{2,1,0:T(8,128)(2,1)S(1)}, bf16[1,128,1536]{2,1,0:T(8,128)(2,1)}, u32[]{:S(2)}) copy-start(bf16[1,128,1536]{2,1,0:T(8,128)(2,1)} %param.15) | copy-start | bytes 1179652
  535.3 6.2 %copy-start.14 = (f32[1,128,1536]{2,1,0:T(8,128)S(1)}, f32[1,128,1536]{2,1,0:T(8,128)}, u32[]{:S(2)}) copy-start(f32[1,128,1536]{2,1,0:T(8,128)} %copy.155) | copy-start | bytes 2359300
  541.5 2.6 copy-start.2
  541.5 2.6 copy-start.1
where the time goes:
time: 546 us; the launch traced here: 544 us
  blocking collectives  238 us (44%)
  waiting for transfers between devices  98 us (18%)
  matrix products  75 us (14%)
  local copies, waits for them, and re-layouts  68.1 us (12%)
  starting transfers between devices  34.3 us (6%)
  other arithmetic  28 us (5%)
    psum x1, blocking collectives, on_device(): gain_grad = lax.psum(jnp.stack([query_term, key_term]), ('dp', 'ctx'))  100 us
    all_to_all x3, waiting for transfers between devices, on_device(): lax.all_to_all(for_sending(outputs), 'ctx', split_axis=2, concat_axis=2,...  64.1 us
    all_to_all x1, blocking collectives, on_device(): lax.all_to_all(outgoing[0], 'ctx', split_axis=2, concat_axis=2, tiled=True)  52 us
    all_to_all x1, blocking collectives, on_device(): lax.all_to_all(outgoing[2], 'ctx', split_axis=2, concat_axis=2, tiled=True)  43.4 us
    all_to_all x1, blocking collectives, on_device(): lax.all_to_all(outgoing[1], 'ctx', split_axis=2, concat_axis=2, tiled=True)  42.8 us
    all_to_all x1, waiting for transfers between devices, on_device(): lax.all_to_all(outgoing[3], 'ctx', split_axis=2, concat_axis=2, tiled=True)  33.9 us
    scatter x3, local copies, waits for them, and re-layouts, unpack_rows(): placed = jnp.zeros((part_count * tile_count, per_tile, item_count, head_d...  30.1 us
    all_to_all x3, starting transfers between devices, on_device(): lax.all_to_all(for_sending(outputs), 'ctx', split_axis=2, concat_axis=2,...  28 us
  transfers between devices with their start and end apart: 4, of which 3 were waited for; matrix products, arithmetic and copies ran while one was open for 9% of the time, Pallas kernels for 0%

commit v1 on v0

v1 whole, which is shorter than its diff:
```python
import math

import jax
import jax.numpy as jnp
from jax import lax
from jax.experimental import pallas as pl
from jax.experimental.pallas import tpu as pltpu
from jax.sharding import PartitionSpec as P

epsilon = 1e-06

GROUPS = 4
SLOTS = 2
PIECE_ROWS = 8
HEAD_DIM = 128


def packed_places(image_ref, tile_count):
    images = [image_ref[0, t] for t in range(tile_count)]
    one = jnp.int32(1)
    zero = jnp.int32(0)
    joined = [zero] + [
        jnp.where(images[t] == images[t - 1], one, zero) for t in range(1, tile_count)
    ]
    long_count = sum(joined[1:], zero)
    long_next = zero
    short_next = long_count * 2
    places = []
    for t in range(tile_count):
        ahead = joined[t + 1] if t + 1 < tile_count else zero
        in_long = joined[t] + ahead
        places.append(jnp.where(in_long > 0, long_next, short_next))
        long_next = long_next + in_long
        short_next = short_next + (1 - in_long)
    return places, long_count


def pack_kernel(image_ref, *refs):
    sources, out_ref = refs[:-1], refs[-1]
    tile_count = sources[0].shape[0]
    heads = sources[0].shape[2] // HEAD_DIM
    per_group = heads // GROUPS
    places, _ = packed_places(image_ref, tile_count)
    for t in range(tile_count):
        pair = places[t] // SLOTS
        slot = places[t] % SLOTS
        for a, source in enumerate(sources):
            for c in range(heads):
                out_ref[
                    pair * GROUPS + c // per_group,
                    (a * per_group + c % per_group) * SLOTS + slot,
                ] = source[t, :, c * HEAD_DIM : (c + 1) * HEAD_DIM]


def unpack_kernel(image_ref, blocks_ref, *outs):
    tile_count = outs[0].shape[0]
    heads = outs[0].shape[2] // HEAD_DIM
    per_group = heads // GROUPS
    places, _ = packed_places(image_ref, tile_count)
    for t in range(tile_count):
        pair = places[t] // SLOTS
        slot = places[t] % SLOTS
        for a, out in enumerate(outs):
            for c in range(heads):
                out[t, :, c * HEAD_DIM : (c + 1) * HEAD_DIM] = blocks_ref[
                    pair * GROUPS + c // per_group,
                    (a * per_group + c % per_group) * SLOTS + slot,
                ]


def work_kernel(per_group, place_ref, image_ref, gains_ref, blocks_ref, out_ref):
    shards = blocks_ref.shape[0]
    tile_count = image_ref.shape[1]
    rows = shards * SLOTS * PIECE_ROWS
    scale = 1.0 / math.sqrt(HEAD_DIM)
    f32, bf16 = jnp.float32, jnp.bfloat16
    _, long_count = packed_places(image_ref, tile_count)
    is_long = place_ref[0] // GROUPS < long_count

    period = SLOTS * PIECE_ROWS
    key_slot = lax.broadcasted_iota(jnp.int32, (period, rows), 0) // PIECE_ROWS % SLOTS
    query_slot = lax.broadcasted_iota(jnp.int32, (period, rows), 1) // PIECE_ROWS % SLOTS
    apart = jnp.where(is_long, 0.0, -1e30).astype(f32)
    bias = jnp.where(key_slot == query_slot, jnp.zeros((), f32), apart)

    def load(a, h):
        first = (a * per_group + h) * SLOTS
        return blocks_ref[:, first : first + SLOTS].astype(f32).reshape(rows, HEAD_DIM)

    def store(a, h, value):
        first = (a * per_group + h) * SLOTS
        out_ref[:, first : first + SLOTS] = value.reshape(
            shards, SLOTS, PIECE_ROWS, HEAD_DIM
        ).astype(bf16)

    def normalize(raw, gain):
        inverse = lax.rsqrt(jnp.mean(raw * raw, axis=-1, keepdims=True) + epsilon)
        unit = raw * inverse
        return unit, inverse, (unit * gain).astype(bf16)

    def norm_back(grad_norm, unit, inverse, gain):
        grad = grad_norm.astype(bf16).astype(f32)
        direct = grad * gain
        inner = jnp.mean(direct * unit, axis=-1, keepdims=True)
        return inverse * (direct - unit * inner), jnp.sum(grad * unit, axis=0, keepdims=True)

    def dot(a, b, dims):
        return lax.dot_general(a, b, (dims, ((), ())), preferred_element_type=f32)

    query_gain = gains_ref[0:1, :]
    key_gain = gains_ref[1:2, :]
    query_term = jnp.zeros((1, HEAD_DIM), f32)
    key_term = jnp.zeros((1, HEAD_DIM), f32)
    for h in range(per_group):
        query_unit, query_inverse, query_norm = normalize(load(0, h), query_gain)
        key_unit, key_inverse, key_norm = normalize(load(1, h), key_gain)
        value = load(2, h).astype(bf16)
        grad = load(3, h).astype(bf16)
        scores = dot(key_norm, query_norm, ((1,), (1,)))
        scores = (scores.reshape(shards, period, rows) + bias[None]).reshape(rows, rows)
        top = jnp.max(scores, axis=0, keepdims=True)
        powers = jnp.exp((scores - top) * scale)
        weights = powers * (1.0 / jnp.sum(powers, axis=0, keepdims=True))
        weight_grad = dot(value, grad, ((1,), (1,)))
        row_inner = jnp.sum(weights * weight_grad, axis=0, keepdims=True)
        score_grad = (weights * (weight_grad - row_inner)).astype(bf16)
        value_grad = dot(weights.astype(bf16), grad, ((1,), (0,)))
        key_norm_grad = dot(score_grad, query_norm, ((1,), (0,))) * scale
        query_norm_grad = dot(score_grad, key_norm, ((0,), (0,))) * scale
        query_grad, term = norm_back(query_norm_grad, query_unit, query_inverse, query_gain)
        query_term = query_term + term
        key_grad, term = norm_back(key_norm_grad, key_unit, key_inverse, key_gain)
        key_term = key_term + term
        store(0, h, query_grad)
        store(1, h, key_grad)
        store(2, h, value_grad)

    terms = jnp.concatenate([query_term, key_term], axis=0)
    parts = []
    for _ in range(3):
        part = terms.astype(bf16).astype(f32)
        parts.append(part)
        terms = terms - part
    parts.append(jnp.zeros_like(terms))
    piece = jnp.concatenate(parts, axis=0).astype(bf16)
    last = out_ref.shape[1] - 1
    out_ref[:, last] = jnp.broadcast_to(piece[None], (shards,) + piece.shape)


SMEM = pl.BlockSpec(memory_space=pltpu.SMEM)
VMEM = pl.BlockSpec(memory_space=pltpu.VMEM)
PARAMS = pltpu.CompilerParams(vmem_limit_bytes=40 * 1024 * 1024)


def on_device(queries, keys, values, out_grad, norm_gains, tile_image):
    shards = lax.axis_size("ctx")
    replicas = lax.axis_size("dp")
    place = lax.axis_index("ctx").astype(jnp.int32).reshape(1)
    token_rows, width = queries.shape[1:]
    tile_count = tile_image.shape[1]
    per_group = width // (GROUPS * HEAD_DIM)
    per_array = per_group * SLOTS
    tiled = (tile_count, PIECE_ROWS, width)

    sources = [x.reshape(tiled) for x in (queries, keys, values, out_grad)]
    packed = pl.pallas_call(
        pack_kernel,
        out_shape=jax.ShapeDtypeStruct(
            (shards, 4 * per_array, PIECE_ROWS, HEAD_DIM), jnp.bfloat16
        ),
        in_specs=[SMEM] + [VMEM] * 4,
        out_specs=VMEM,
        compiler_params=PARAMS,
        name="pack",
    )(tile_image, *sources)
    arrived = lax.all_to_all(packed, "ctx", split_axis=0, concat_axis=0, tiled=True)

    def body(*refs):
        work_kernel(per_group, *refs)

    worked = pl.pallas_call(
        body,
        out_shape=jax.ShapeDtypeStruct(
            (shards, 3 * per_array + 1, PIECE_ROWS, HEAD_DIM), jnp.bfloat16
        ),
        in_specs=[SMEM, SMEM, VMEM, VMEM],
        out_specs=VMEM,
        compiler_params=PARAMS,
        name="work",
    )(place, tile_image, norm_gains, arrived)
    returned = lax.all_to_all(worked, "ctx", split_axis=0, concat_axis=0, tiled=True)

    pieces = jnp.sum(returned[:, 3 * per_array, :6].astype(jnp.float32), axis=0)
    own_terms = jnp.sum(pieces.reshape(3, 2, HEAD_DIM), axis=0)
    all_terms = lax.all_to_all(
        jnp.broadcast_to(own_terms[None], (replicas, 2, HEAD_DIM)),
        "dp",
        split_axis=0,
        concat_axis=0,
        tiled=True,
    )
    gain_grad = jnp.sum(all_terms, axis=0)

    grads = pl.pallas_call(
        unpack_kernel,
        out_shape=[jax.ShapeDtypeStruct(tiled, jnp.bfloat16)] * 3,
        in_specs=[SMEM, VMEM],
        out_specs=[VMEM] * 3,
        compiler_params=PARAMS,
        name="unpack",
    )(tile_image, returned)
    grads = [x.reshape(1, token_rows, width) for x in grads]
    return (grads[0], grads[1], grads[2], gain_grad)


def solution(mesh):
    rows = P("dp", "ctx", None)
    in_specs = (rows, rows, rows, rows, P(), P("dp", None))
    out_specs = (rows, rows, rows, P())
    return jax.shard_map(
        on_device, mesh=mesh, in_specs=in_specs, out_specs=out_specs, check_vma=False
    )
```

time: 546 us -> 120 us (0.22)
  blocking collectives: 238 us -> 36.7 us
  matrix products: 75 us -> 0 us
  local copies, waits for them, and re-layouts: 68.1 us -> 5.25 us
  waiting for transfers between devices: 98 us -> 43.4 us
  other arithmetic: 28 us -> 0.64 us
  starting transfers between devices: 34.3 us -> 25 us
  Pallas kernels: 0 us -> 7.97 us
    all_to_all x3 -> x1, blocking collectives: 138 us -> 36.7 us  [on_device(): lax.all_to_all(worked, 'ctx', split_axis=0, concat_axis=0, tiled=True)]
    psum x1 -> x0, blocking collectives: 100 us -> none  [on_device(): gain_grad = lax.psum(jnp.stack([query_term, key_term]), ('dp', 'ctx'))]
    dot_general x60 -> x0, matrix products: 75 us -> none  [the longest x12 22.3 us: head_grads(): jnp.einsum('qk,qd->kd', score_grad, query_rows, preferred_element_type=jn...]
    all_to_all x4 -> x2, waiting for transfers between devices: 98 us -> 43.4 us  [the longest x1 37.9 us: on_device(): lax.all_to_all(packed, 'ctx', split_axis=0, concat_axis=0, tiled=True)]
    scatter x3 -> x0, local copies, waits for them, and re-layouts: 30.1 us -> none  [unpack_rows(): placed = jnp.zeros((part_count * tile_count, per_tile, item_count, head_d...]
    convert_element_type x18 -> x0, other arithmetic: 10.7 us -> none  [the longest x2 3.51 us: norm_back(): result.reshape(unit_rows.shape[0], -1).astype(jnp.bfloat16)]
    cond x5 -> x0, local copies, waits for them, and re-layouts: 9.51 us -> none  [the longest x3 9.51 us: on_device(): lax.cond(own_flag, whole_image, paired, (lax.all_to_all(outgoing[0], 'ctx...]
    all_to_all x4 -> x2, starting transfers between devices: 34.3 us -> 25 us  [the longest x1 13.8 us: on_device(): lax.all_to_all(packed, 'ctx', split_axis=0, concat_axis=0, tiled=True)]
  transfers between devices with their start and end apart: 4 -> 2, of which waited for: 3 -> 2; matrix products, arithmetic and copies ran while one was open for 9% -> 0% of each run, Pallas kernels for 0% -> 2%
where the time goes in v1:
time: 120 us
  waiting for transfers between devices  43.4 us (36%)
  blocking collectives  36.7 us (31%)
  starting transfers between devices  25 us (21%)
  Pallas kernels  7.97 us (7%)
  local copies, waits for them, and re-layouts  5.25 us (4%)
    all_to_all x1, waiting for transfers between devices, on_device(): lax.all_to_all(packed, 'ctx', split_axis=0, concat_axis=0, tiled=True)  37.9 us
    all_to_all x1, blocking collectives, on_device(): lax.all_to_all(worked, 'ctx', split_axis=0, concat_axis=0, tiled=True)  36.7 us
    all_to_all x1, starting transfers between devices, on_device(): lax.all_to_all(packed, 'ctx', split_axis=0, concat_axis=0, tiled=True)  13.8 us
    all_to_all x1, starting transfers between devices, on_device(): lax.all_to_all(jnp.broadcast_to(own_terms[None], (replicas, 2, HEAD_DIM))...  11.1 us
    all_to_all x1, waiting for transfers between devices, on_device(): lax.all_to_all(jnp.broadcast_to(own_terms[None], (replicas, 2, HEAD_DIM))...  5.5 us
    unnamed x14, local copies, waits for them, and re-layouts  4.64 us
    pallas_call x1, Pallas kernels, on_device(): pl.pallas_call(body, out_shape=jax.ShapeDtypeStruct((shards, 3 * per_arra...  4.06 us
  transfers between devices with their start and end apart: 2, of which 2 were waited for; matrix products, arithmetic and copies ran while one was open for 0% of the time, Pallas kernels for 2%

profile of v1, /device:TPU:1, one launch (start us, length us, event | category | flops | bytes accessed | tf_op | source)
XLA Modules:
  0.0 119.6 jit_solution(2017608513193100602)
XLA Ops:
  0.6 0.0 copy-start
  0.6 1.0 copy-done
  1.6 0.0 copy-start.1
  1.6 1.0 copy-done.1
  2.6 0.0 copy-start.2
  2.6 1.0 copy-done.2
  3.6 0.0 copy-start.3
  3.6 1.0 copy-done.3
  4.6 0.0 copy-start.4
  4.6 0.7 copy-done.4
  5.3 2.1 %pack.1 = bf16[32,24,8,128]{3,2,1,0:T(8,128)(2,1)} custom-call(s32[1,16]{1,0:T(1,128)S(1)} %copy-done.4, bf16[16,8,1536]{2,1,0:T(8,128)(2,1)S(1)} %bitcast.8, bf16[16,8,1536]{2,1,0:T(8,128)(2,1)S(1)} %bitcast.9, bf16[16,8,1536]{2,1,0:T(8,128)(2,1)S(1)} %bitcast.10, bf16[16,8,1536]{2,1,0:T(8,128)(2,1)S(1)} %bitcast.11), custom_call_target="tpu_custom_call" | custom-call | tf_op jit(solution)/shard_map/pack/pallas_call | solution.py:166
  7.3 0.0 copy-start.5
  7.3 0.0 copy-start.6
  7.3 13.8 %all-to-all-start = ((bf16[32,24,8,128]{3,2,1,0:T(8,128)(2,1)}), bf16[32,24,8,128]{3,2,1,0:T(8,128)(2,1)S(1)}, u32[]{:S(2)}, u32[]{:S(2)}) async-start(bf16[32,24,8,128]{3,2,1,0:T(8,128)(2,1)} %pack.1), calls=%async_computation | async-start | bytes 3145728 | tf_op jit(solution)/shard_map/all_to_all | solution.py:176
  21.2 37.9 %all-to-all-done.refs_3_ = bf16[32,24,8,128]{3,2,1,0:T(8,128)(2,1)S(1)} async-done(((bf16[32,24,8,128]{3,2,1,0:T(8,128)(2,1)}), bf16[32,24,8,128]{3,2,1,0:T(8,128)(2,1)S(1)}, u32[]{:S(2)}, u32[]{:S(2)}) %all-to-all-start) | async-done | bytes 1572896 | tf_op jit(solution)/shard_map/all_to_all | solution.py:176
  59.1 0.0 copy-done.5
  59.1 0.0 copy-done.6
  59.1 4.1 %work.1 = bf16[32,19,8,128]{3,2,1,0:T(8,128)(2,1)S(1)} custom-call(s32[1]{0:T(128)} %bitcast.refs_0_, s32[1,16]{1,0:T(1,128)S(1)} %copy-done.5, f32[2,128]{1,0:T(2,128)S(1)} %copy-done.6, bf16[32,24,8,128]{3,2,1,0:T(8,128)(2,1)S(1)} %all-to-all-done.refs_3_), custom_call_target="tpu_custom_call" | custom-call | tf_op jit(solution)/shard_map/work/pallas_call | solution.py:181
  63.1 36.7 %all_to_all.15.blocks_ref = bf16[32,19,8,128]{3,2,1,0:T(8,128)(2,1)S(1)} all-to-all(bf16[32,19,8,128]{3,2,1,0:T(8,128)(2,1)S(1)} %work.1), channel_id=1, replica_groups=mesh['dp'=16,'ctx'=32] {'ctx'}, dimensions={0} | all-to-all | bytes 2490368 | tf_op jit(solution)/shard_map/all_to_all | solution.py:191
  99.9 0.6 broadcast_in_dim.2
  100.5 11.1 %all-to-all-start.2 = ((f32[16,2,128]{2,1,0:T(2,128)}), f32[16,2,128]{2,1,0:T(2,128)S(1)}, u32[]{:S(2)}, u32[]{:S(2)}) async-start(f32[16,2,128]{2,1,0:T(2,128)} %broadcast_in_dim.2), calls=%async_computation.2 | async-start | bytes 32768 | tf_op jit(solution)/shard_map/all_to_all | solution.py:195
  111.7 1.8 %unpack.1 = (bf16[16,8,1536]{2,1,0:T(8,128)(2,1)}, bf16[16,8,1536]{2,1,0:T(8,128)(2,1)}, bf16[16,8,1536]{2,1,0:T(8,128)(2,1)}) custom-call(s32[1,16]{1,0:T(1,128)S(1)} %copy-done.5, bf16[32,19,8,128]{3,2,1,0:T(8,128)(2,1)S(1)} %all_to_all.15.blocks_ref), custom_call_target="tpu_custom_call" | custom-call | tf_op jit(solution)/shard_map/unpack/pallas_call | solution.py:204
  113.5 5.5 %all-to-all-done.2 = f32[16,2,128]{2,1,0:T(2,128)S(1)} async-done(((f32[16,2,128]{2,1,0:T(2,128)}), f32[16,2,128]{2,1,0:T(2,128)S(1)}, u32[]{:S(2)}, u32[]{:S(2)}) %all-to-all-start.2) | async-done | bytes 16416 | tf_op jit(solution)/shard_map/all_to_all | solution.py:195
  119.0 0.6 reduce_sum.29
  (3 shorter events, 0.1 us)
Async XLA Ops:
  0.6 1.0 copy-start
  1.6 1.0 copy-start.1
  2.6 1.0 copy-start.2
  3.6 1.0 copy-start.3
  4.6 0.7 copy-start.4
  7.3 51.7 %copy-start.5 = (s32[1,16]{1,0:T(1,128)S(1)}, s32[1,16]{1,0:T(1,128)}, u32[]{:S(2)}) copy-start(s32[1,16]{1,0:T(1,128)} %image_ref.3) | copy-start | bytes 196
  7.3 51.7 %copy-start.6 = (f32[2,128]{1,0:T(2,128)S(1)}, f32[2,128]{1,0:T(2,128)}, u32[]{:S(2)}) copy-start(f32[2,128]{1,0:T(2,128)} %refs_2_.1) | copy-start | bytes 3076
  7.3 51.7 %all-to-all-start = ((bf16[32,24,8,128]{3,2,1,0:T(8,128)(2,1)}), bf16[32,24,8,128]{3,2,1,0:T(8,128)(2,1)S(1)}, u32[]{:S(2)}, u32[]{:S(2)}) async-start(bf16[32,24,8,128]{3,2,1,0:T(8,128)(2,1)} %pack.1), calls=%async_computation | async-start | bytes 3145728 | tf_op jit(solution)/shard_map/all_to_all | solution.py:176
  100.5 18.5 %all-to-all-start.2 = ((f32[16,2,128]{2,1,0:T(2,128)}), f32[16,2,128]{2,1,0:T(2,128)S(1)}, u32[]{:S(2)}, u32[]{:S(2)}) async-start(f32[16,2,128]{2,1,0:T(2,128)} %broadcast_in_dim.2), calls=%async_computation.2 | async-start | bytes 32768 | tf_op jit(solution)/shard_map/all_to_all | solution.py:195

commit v2 on v1

--- a/solution.py
+++ b/solution.py
@@ -13,6 +13,7 @@
 SLOTS = 2
 PIECE_ROWS = 8
 HEAD_DIM = 128
+EARLY = 2
 
 
 def packed_places(image_ref, tile_count):
@@ -35,40 +36,63 @@
     return places, long_count
 
 
-def pack_kernel(image_ref, *refs):
-    sources, out_ref = refs[:-1], refs[-1]
-    tile_count = sources[0].shape[0]
-    heads = sources[0].shape[2] // HEAD_DIM
+def pack_kernel(image_hbm, *refs):
+    sources, out_ref = refs[:4], refs[4]
+    image_ref, held, image_sem, sems = refs[5:]
+    tile_count = held.shape[1]
+    heads = held.shape[3] // HEAD_DIM
     per_group = heads // GROUPS
+    half = tile_count // 2
+    image_copy = pltpu.make_async_copy(image_hbm, image_ref, image_sem)
+    image_copy.start()
+    copies = []
+    for a, source in enumerate(sources):
+        for part in range(2):
+            tiles = pl.ds(part * half, half)
+            copy = pltpu.make_async_copy(source.at[tiles], held.at[a, tiles], sems.at[a, part])
+            copy.start()
+            copies.append(copy)
+    image_copy.wait()
     places, _ = packed_places(image_ref, tile_count)
-    for t in range(tile_count):
-        pair = places[t] // SLOTS
-        slot = places[t] % SLOTS
-        for a, source in enumerate(sources):
+    for a in range(len(sources)):
+        for t in range(tile_count):
+            if t % half == 0:
+                copies[a * 2 + t // half].wait()
+            pair = places[t] // SLOTS
+            slot = places[t] % SLOTS
             for c in range(heads):
                 out_ref[
                     pair * GROUPS + c // per_group,
                     (a * per_group + c % per_group) * SLOTS + slot,
-                ] = source[t, :, c * HEAD_DIM : (c + 1) * HEAD_DIM]
-
-
-def unpack_kernel(image_ref, blocks_ref, *outs):
+                ] = held[a, t, :, c * HEAD_DIM : (c + 1) * HEAD_DIM]
+
+
+def unpack_kernel(image_ref, early_ref, late_ref, *outs):
+    outs, gain_ref = outs[:-1], outs[-1]
     tile_count = outs[0].shape[0]
     heads = outs[0].shape[2] // HEAD_DIM
     per_group = heads // GROUPS
     places, _ = packed_places(image_ref, tile_count)
-    for t in range(tile_count):
-        pair = places[t] // SLOTS
-        slot = places[t] % SLOTS
-        for a, out in enumerate(outs):
+    for a, out in enumerate(outs):
+        for t in range(tile_count):
+            pair = places[t] // SLOTS
+            slot = places[t] % SLOTS
             for c in range(heads):
-                out[t, :, c * HEAD_DIM : (c + 1) * HEAD_DIM] = blocks_ref[
-                    pair * GROUPS + c // per_group,
-                    (a * per_group + c % per_group) * SLOTS + slot,
+                h = c % per_group
+                if h < EARLY:
+                    held, piece = early_ref, (a * EARLY + h) * SLOTS
+                else:
+                    held, piece = late_ref, (a * (per_group - EARLY) + h - EARLY) * SLOTS
+                out[t, :, c * HEAD_DIM : (c + 1) * HEAD_DIM] = held[
+                    pair * GROUPS + c // per_group, piece + slot
                 ]
-
-
-def work_kernel(per_group, place_ref, image_ref, gains_ref, blocks_ref, out_ref):
+    parts = jnp.sum(late_ref[:, late_ref.shape[1] - 1].astype(jnp.float32), axis=0)
+    gain_ref[...] = parts[0:2] + parts[2:4] + parts[4:6]
+
+
+def work_kernel(per_group, heads, place_ref, image_ref, gains_ref, blocks_ref, *refs):
+    before_ref = refs[0] if len(refs) == 3 else None
+    out_ref, terms_ref = refs[-2:]
     shards = blocks_ref.shape[0]
     tile_count = image_ref.shape[1]
     rows = shards * SLOTS * PIECE_ROWS
@@ -88,7 +112,7 @@
         return blocks_ref[:, first : first + SLOTS].astype(f32).reshape(rows, HEAD_DIM)
 
     def store(a, h, value):
-        first = (a * per_group + h) * SLOTS
+        first = (a * len(heads) + h - heads[0]) * SLOTS
         out_ref[:, first : first + SLOTS] = value.reshape(
             shards, SLOTS, PIECE_ROWS, HEAD_DIM
         ).astype(bf16)
@@ -111,7 +135,7 @@
     key_gain = gains_ref[1:2, :]
     query_term = jnp.zeros((1, HEAD_DIM), f32)
     key_term = jnp.zeros((1, HEAD_DIM), f32)
-    for h in range(per_group):
+    for h in heads:
         query_unit, query_inverse, query_norm = normalize(load(0, h), query_gain)
         key_unit, key_inverse, key_norm = normalize(load(1, h), key_gain)
         value = load(2, h).astype(bf16)
@@ -136,79 +160,116 @@
         store(2, h, value_grad)
 
     terms = jnp.concatenate([query_term, key_term], axis=0)
+    if before_ref is not None:
+        terms = terms + before_ref[...]
+    terms_ref[...] = terms
+
+
+def attach_kernel(terms_ref, blocks_ref, out_ref):
+    last = blocks_ref.shape[1]
+    out_ref[:, :last] = blocks_ref[...]
+    terms = terms_ref[...]
     parts = []
     for _ in range(3):
-        part = terms.astype(bf16).astype(f32)
+        part = terms.astype(jnp.bfloat16).astype(jnp.float32)
         parts.append(part)
         terms = terms - part
     parts.append(jnp.zeros_like(terms))
-    piece = jnp.concatenate(parts, axis=0).astype(bf16)
-    last = out_ref.shape[1] - 1
-    out_ref[:, last] = jnp.broadcast_to(piece[None], (shards,) + piece.shape)
+    piece = jnp.concatenate(parts, axis=0).astype(jnp.bfloat16)
+    out_ref[:, last] = jnp.broadcast_to(piece[None], out_ref[:, last].shape)
 
 
 SMEM = pl.BlockSpec(memory_space=pltpu.SMEM)
 VMEM = pl.BlockSpec(memory_space=pltpu.VMEM)
-PARAMS = pltpu.CompilerParams(vmem_limit_bytes=40 * 1024 * 1024)
+HBM = pl.BlockSpec(memory_space=pltpu.HBM)
+
+
+def params(mib):
+    return pltpu.CompilerParams(vmem_limit_bytes=mib * 1024 * 1024)
+
+
+def exchange(blocks):
+    return lax.all_to_all(blocks, "ctx", split_axis=0, concat_axis=0, tiled=True)
 
 
 def on_device(queries, keys, values, out_grad, norm_gains, tile_image):
+    bf16, f32 = jnp.bfloat16, jnp.float32
     shards = lax.axis_size("ctx")
     replicas = lax.axis_size("dp")
     place = lax.axis_index("ctx").astype(jnp.int32).reshape(1)
     token_rows, width = queries.shape[1:]
     tile_count = tile_image.shape[1]
     per_group = width // (GROUPS * HEAD_DIM)
-    per_array = per_group * SLOTS
     tiled = (tile_count, PIECE_ROWS, width)
+
+    def blocks(pieces):
+        return jax.ShapeDtypeStruct((shards, pieces, PIECE_ROWS, HEAD_DIM), bf16)
 
     sources = [x.reshape(tiled) for x in (queries, keys, values, out_grad)]
     packed = pl.pallas_call(
         pack_kernel,
-        out_shape=jax.ShapeDtypeStruct(
-            (shards, 4 * per_array, PIECE_ROWS, HEAD_DIM), jnp.bfloat16
-        ),
-        in_specs=[SMEM] + [VMEM] * 4,
+        out_shape=blocks(4 * per_group * SLOTS),
+        in_specs=[HBM] * 5,
         out_specs=VMEM,
-        compiler_params=PARAMS,
+        scratch_shapes=[
+            pltpu.SMEM(tile_image.shape, jnp.int32),
+            pltpu.VMEM((4,) + tiled, bf16),
+            pltpu.SemaphoreType.DMA(()),
+            pltpu.SemaphoreType.DMA((4, 2)),
+        ],
+        compiler_params=params(62),
         name="pack",
     )(tile_image, *sources)
-    arrived = lax.all_to_all(packed, "ctx", split_axis=0, concat_axis=0, tiled=True)
-
-    def body(*refs):
-        work_kernel(per_group, *refs)
-
-    worked = pl.pallas_call(
-        body,
-        out_shape=jax.ShapeDtypeStruct(
-            (shards, 3 * per_array + 1, PIECE_ROWS, HEAD_DIM), jnp.bfloat16
-        ),
-        in_specs=[SMEM, SMEM, VMEM, VMEM],
+    arrived = exchange(packed)
+
+    def work(name, heads, *before):
+        def body(*refs):
+            work_kernel(per_group, heads, *refs)
+
+        return pl.pallas_call(
+            body,
+            out_shape=[
+                blocks(3 * len(heads) * SLOTS),
+                jax.ShapeDtypeStruct(norm_gains.shape, f32),
+            ],
+            in_specs=[SMEM, SMEM, VMEM, VMEM] + [VMEM] * len(before),
+            out_specs=[VMEM, VMEM],
+            compiler_params=params(32),
+            cost_estimate=pl.CostEstimate(
+                flops=len(heads) * 10 * arrived.size // arrived.shape[1] * 512,
+                bytes_accessed=arrived.size * 2,
+                transcendentals=len(heads) * 512 * 512,
+            ),
+            name=name,
+        )(place, tile_image, norm_gains, arrived, *before)
+
+    early, early_terms = work("early", tuple(range(EARLY)))
+    early_back = exchange(early)
+    late, terms = work("late", tuple(range(EARLY, per_group)), early_terms)
+    cores = [[2 * y, 2 * y + 1] for y in range(replicas // 2)]
+    columns = [[2 * y + core for y in range(replicas // 2)] for core in range(2)]
+    terms = lax.psum(terms, "dp", axis_index_groups=cores)
+    terms = lax.psum(terms, "dp", axis_index_groups=columns)
+    late = pl.pallas_call(
+        attach_kernel,
+        out_shape=blocks(late.shape[1] + 1),
+        in_specs=[VMEM, VMEM],
         out_specs=VMEM,
-        compiler_params=PARAMS,
-        name="work",
-    )(place, tile_image, norm_gains, arrived)
-    returned = lax.all_to_all(worked, "ctx", split_axis=0, concat_axis=0, tiled=True)
-
-    pieces = jnp.sum(returned[:, 3 * per_array, :6].astype(jnp.float32), axis=0)
-    own_terms = jnp.sum(pieces.reshape(3, 2, HEAD_DIM), axis=0)
-    all_terms = lax.all_to_all(
-        jnp.broadcast_to(own_terms[None], (replicas, 2, HEAD_DIM)),
-        "dp",
-        split_axis=0,
-        concat_axis=0,
-        tiled=True,
-    )
-    gain_grad = jnp.sum(all_terms, axis=0)
-
-    grads = pl.pallas_call(
+        compiler_params=params(8),
+        name="attach",
+    )(terms, late)
+    early_back, late = lax.optimization_barrier((early_back, late))
+    late_back = exchange(late)
+
+    *grads, gain_grad = pl.pallas_call(
         unpack_kernel,
-        out_shape=[jax.ShapeDtypeStruct(tiled, jnp.bfloat16)] * 3,
-        in_specs=[SMEM, VMEM],
-        out_specs=[VMEM] * 3,
-        compiler_params=PARAMS,
+        out_shape=[jax.ShapeDtypeStruct(tiled, bf16)] * 3
+        + [jax.ShapeDtypeStruct(norm_gains.shape, f32)],
+        in_specs=[SMEM, VMEM, VMEM],
+        out_specs=[VMEM] * 4,
+        compiler_params=params(16),
         name="unpack",
-    )(tile_image, returned)
+    )(tile_image, early_back, late_back)
     grads = [x.reshape(1, token_rows, width) for x in grads]
     return (grads[0], grads[1], grads[2], gain_grad)
 

time: 120 us -> 112 us (0.933)
  the two profiles are of different devices: /device:TPU:1 before, /device:TPU:2 now
where the time goes in v2:
time: 112 us
  blocking collectives  42.4 us (38%)
  waiting for transfers between devices  38.4 us (34%)
  starting transfers between devices  20 us (18%)
  Pallas kernels  10.6 us (9%)
    all_to_all x2, waiting for transfers between devices, exchange(): lax.all_to_all(blocks, 'ctx', split_axis=0, concat_axis=0, tiled=True)  38.4 us
    all_to_all x1, blocking collectives, exchange(): lax.all_to_all(blocks, 'ctx', split_axis=0, concat_axis=0, tiled=True)  22.3 us
    all_to_all x2, starting transfers between devices, exchange(): lax.all_to_all(blocks, 'ctx', split_axis=0, concat_axis=0, tiled=True)  20 us
    psum x1, blocking collectives, on_device(): terms = lax.psum(terms, 'dp', axis_index_groups=columns)  17.6 us
    pallas_call x2, Pallas kernels, work(): pl.pallas_call(body, out_shape=[blocks(3 * len(heads) * SLOTS), jax.Shape...  5.96 us
    pallas_call x1, Pallas kernels, on_device(): pl.pallas_call(pack_kernel, out_shape=blocks(4 * per_group * SLOTS), in_s...  2.74 us
    psum x1, blocking collectives, on_device(): terms = lax.psum(terms, 'dp', axis_index_groups=cores)  2.47 us
  transfers between devices with their start and end apart: 2, of which 1 were waited for; matrix products, arithmetic and copies ran while one was open for 0% of the time, Pallas kernels for 2%

profile of v2, /device:TPU:2, one launch (start us, length us, event | category | flops | bytes accessed | tf_op | source)
XLA Modules:
  0.0 112.0 jit_solution(5485752344756054039)
XLA Ops:
  0.6 2.7 %pack.1 = bf16[32,24,8,128]{3,2,1,0:T(8,128)(2,1)} custom-call(s32[1,16]{1,0:T(1,128)} %image_ref.1, bf16[16,8,1536]{2,1,0:T(8,128)(2,1)} %bitcast.8, bf16[16,8,1536]{2,1,0:T(8,128)(2,1)} %bitcast.9, bf16[16,8,1536]{2,1,0:T(8,128)(2,1)} %bitcast.10, bf16[16,8,1536]{2,1,0:T(8,128)(2,1)} %bitcast.11), custom_call_target="tpu_custom_call" | custom-call | tf_op jit(solution)/shard_map/pack/pallas_call | solution.py:209
  3.4 0.0 copy-start
  3.4 0.0 copy-start.1
  3.4 13.5 %all-to-all-start = ((bf16[32,24,8,128]{3,2,1,0:T(8,128)(2,1)}), bf16[32,24,8,128]{3,2,1,0:T(8,128)(2,1)S(1)}, u32[]{:S(2)}, u32[]{:S(2)}) async-start(bf16[32,24,8,128]{3,2,1,0:T(8,128)(2,1)} %pack.1), calls=%async_computation | async-start | bytes 3145728 | tf_op jit(solution)/shard_map/all_to_all | solution.py:192
  16.9 38.3 %all-to-all-done.refs_3_ = bf16[32,24,8,128]{3,2,1,0:T(8,128)(2,1)S(1)} async-done(((bf16[32,24,8,128]{3,2,1,0:T(8,128)(2,1)}), bf16[32,24,8,128]{3,2,1,0:T(8,128)(2,1)S(1)}, u32[]{:S(2)}, u32[]{:S(2)}) %all-to-all-start) | async-done | bytes 1572896 | tf_op jit(solution)/shard_map/all_to_all | solution.py:192
  55.2 0.0 copy-done
  55.2 0.0 copy-done.1
  55.2 3.9 %early.1 = (bf16[32,12,8,128]{3,2,1,0:T(8,128)(2,1)}, f32[2,128]{1,0:T(2,128)S(1)}) custom-call(s32[1]{0:T(128)} %bitcast.refs_0_, s32[1,16]{1,0:T(1,128)S(1)} %copy-done, f32[2,128]{1,0:T(2,128)S(1)} %copy-done.1, bf16[32,24,8,128]{3,2,1,0:T(8,128)(2,1)S(1)} %all-to-all-done.refs_3_), custom_call_target="tpu_custom_call" | custom-call | flops 335544320 | bytes 1572864 | tf_op jit(solution)/shard_map/early/pallas_call | solution.py:229
  59.2 6.5 %all-to-all-start.1 = ((bf16[32,12,8,128]{3,2,1,0:T(8,128)(2,1)}), bf16[32,12,8,128]{3,2,1,0:T(8,128)(2,1)S(1)}, u32[]{:S(2)}, u32[]{:S(2)}) async-start(bf16[32,12,8,128]{3,2,1,0:T(8,128)(2,1)} %get-tuple-element.14), calls=%async_computation.1 | async-start | bytes 1572864 | tf_op jit(solution)/shard_map/all_to_all | solution.py:192
  65.7 2.0 %late.1 = (bf16[32,6,8,128]{3,2,1,0:T(8,128)(2,1)S(1)}, f32[2,128]{1,0:T(2,128)S(1)}) custom-call(s32[1]{0:T(128)} %bitcast.refs_0_, s32[1,16]{1,0:T(1,128)S(1)} %copy-done, f32[2,128]{1,0:T(2,128)S(1)} %copy-done.1, bf16[32,24,8,128]{3,2,1,0:T(8,128)(2,1)S(1)} %all-to-all-done.refs_3_, f32[2,128]{1,0:T(2,128)S(1)} %get-tuple-element.15.refs_4_), custom_call_target="tpu_custom_call" | custom-call | flops 167772160 | bytes 1572864 | tf_op jit(solution)/shard_map/late/pallas_call | solution.py:229
  67.7 2.5 %psum.14 = f32[2,128]{1,0:T(2,128)S(1)} all-reduce(f32[2,128]{1,0:T(2,128)S(1)} %get-tuple-element.16), channel_id=1, replica_groups={{0,32},{64,96},{128,160},{192,224},{256,288},{320,352},{384,416},{448,4..., use_global_device_ids=true, to_apply=%region_0.0 | all-reduce | flops 256 | bytes 2048 | tf_op jit(solution)/shard_map/psum | solution.py:251
  70.2 17.6 %psum.15.terms_ref = f32[2,128]{1,0:T(2,128)S(1)} all-reduce(f32[2,128]{1,0:T(2,128)S(1)} %psum.14), channel_id=1, replica_groups={{0,64,128,192,256,320,384,448},{32,96,160,224,288,352,416,480},{1,65,12..., use_global_device_ids=true, to_apply=%region_1.0 | all-reduce | flops 256 | bytes 2048 | tf_op jit(solution)/shard_map/psum | solution.py:252
  87.8 0.0 all-to-all-done.1.early_ref
  87.9 22.3 %all_to_all.15.late_ref = bf16[32,7,8,128]{3,2,1,0:T(8,128)(2,1)S(1)} all-to-all(bf16[32,7,8,128]{3,2,1,0:T(8,128)(2,1)S(1)} %attach.1), channel_id=1, replica_groups=mesh['dp'=16,'ctx'=32] {'ctx'}, dimensions={0} | all-to-all | bytes 917504 | tf_op jit(solution)/shard_map/all_to_all | solution.py:192
  110.2 1.9 %unpack.1 = (bf16[16,8,1536]{2,1,0:T(8,128)(2,1)}, bf16[16,8,1536]{2,1,0:T(8,128)(2,1)}, bf16[16,8,1536]{2,1,0:T(8,128)(2,1)}, f32[2,128]{1,0:T(2,128)}) custom-call(s32[1,16]{1,0:T(1,128)S(1)} %copy-done, bf16[32,12,8,128]{3,2,1,0:T(8,128)(2,1)S(1)} %all-to-all-done.1.early_ref, bf16[32,7,8,128]{3,2,1,0:T(8,128)(2,1)S(1)} %all_to_all.15.late_ref), custom_call_target="tpu_custom_call" | custom-call | tf_op jit(solution)/shard_map/unpack/pallas_call | solution.py:264
  (1 shorter events, 0.0 us)
Async XLA Ops:
  3.4 51.9 %copy-start = (s32[1,16]{1,0:T(1,128)S(1)}, s32[1,16]{1,0:T(1,128)}, u32[]{:S(2)}) copy-start(s32[1,16]{1,0:T(1,128)} %image_ref.1) | copy-start | bytes 196
  3.4 51.9 %copy-start.1 = (f32[2,128]{1,0:T(2,128)S(1)}, f32[2,128]{1,0:T(2,128)}, u32[]{:S(2)}) copy-start(f32[2,128]{1,0:T(2,128)} %refs_2_.3) | copy-start | bytes 3076
  3.4 51.8 %all-to-all-start = ((bf16[32,24,8,128]{3,2,1,0:T(8,128)(2,1)}), bf16[32,24,8,128]{3,2,1,0:T(8,128)(2,1)S(1)}, u32[]{:S(2)}, u32[]{:S(2)}) async-start(bf16[32,24,8,128]{3,2,1,0:T(8,128)(2,1)} %pack.1), calls=%async_computation | async-start | bytes 3145728 | tf_op jit(solution)/shard_map/all_to_all | solution.py:192
  59.2 28.7 %all-to-all-start.1 = ((bf16[32,12,8,128]{3,2,1,0:T(8,128)(2,1)}), bf16[32,12,8,128]{3,2,1,0:T(8,128)(2,1)S(1)}, u32[]{:S(2)}, u32[]{:S(2)}) async-start(bf16[32,12,8,128]{3,2,1,0:T(8,128)(2,1)} %get-tuple-element.14), calls=%async_computation.1 | async-start | bytes 1572864 | tf_op jit(solution)/shard_map/all_to_all | solution.py:192

commit v3 on v2

v3 whole, which is shorter than its diff:
```python
import functools
import math

import jax
import jax.numpy as jnp
from jax import lax
from jax.experimental import pallas as pl
from jax.experimental.pallas import tpu as pltpu
from jax.sharding import PartitionSpec as P

epsilon = 1e-06

GROUPS = 4
SLOTS = 2
PIECE_ROWS = 8
HEAD_DIM = 128
PLANS = (((0, 1, 2),), ((0,), (1, 2)))
BACK = ((0,), (1, 2))


def packed_places(image_ref, tile_count):
    images = [image_ref[0, t] for t in range(tile_count)]
    one = jnp.int32(1)
    zero = jnp.int32(0)
    joined = [zero] + [
        jnp.where(images[t] == images[t - 1], one, zero) for t in range(1, tile_count)
    ]
    long_count = sum(joined[1:], zero)
    long_next = zero
    short_next = long_count * 2
    places = []
    for t in range(tile_count):
        ahead = joined[t + 1] if t + 1 < tile_count else zero
        in_long = joined[t] + ahead
        places.append(jnp.where(in_long > 0, long_next, short_next))
        long_next = long_next + in_long
        short_next = short_next + (1 - in_long)
    return places, long_count


def chunk_of(chunks):
    return {h: (i, chunk.index(h)) for i, chunk in enumerate(chunks) for h in chunk}


def pack_kernel(chunks, image_hbm, *refs):
    sources, outs = refs[:4], refs[4 : 4 + len(chunks)]
    image_ref, held, image_sem, sems = refs[4 + len(chunks) :]
    tile_count = held.shape[1]
    heads = held.shape[3] // HEAD_DIM
    per_group = heads // GROUPS
    half = tile_count // 2
    where = chunk_of(chunks)
    image_copy = pltpu.make_async_copy(image_hbm, image_ref, image_sem)
    image_copy.start()
    copies = []
    for a, source in enumerate(sources):
        for part in range(2):
            tiles = pl.ds(part * half, half)
            copy = pltpu.make_async_copy(source.at[tiles], held.at[a, tiles], sems.at[a, part])
            copy.start()
            copies.append(copy)
    image_copy.wait()
    places, _ = packed_places(image_ref, tile_count)
    for a in range(len(sources)):
        for t in range(tile_count):
            if t % half == 0:
                copies[a * 2 + t // half].wait()
            pair = places[t] // SLOTS
            slot = places[t] % SLOTS
            for c in range(heads):
                chunk, position = where[c % per_group]
                outs[chunk][
                    pair * GROUPS + c // per_group,
                    (a * len(chunks[chunk]) + position) * SLOTS + slot,
                ] = held[a, t, :, c * HEAD_DIM : (c + 1) * HEAD_DIM]


def unpack_kernel(image_ref, *refs):
    blocks, outs = refs[: len(BACK)], refs[len(BACK) :]
    tile_count = outs[0].shape[0]
    heads = outs[0].shape[2] // HEAD_DIM
    per_group = heads // GROUPS
    where = chunk_of(BACK)
    places, _ = packed_places(image_ref, tile_count)
    for a, out in enumerate(outs):
        for t in range(tile_count):
            pair = places[t] // SLOTS
            slot = places[t] % SLOTS
            for c in range(heads):
                chunk, position = where[c % per_group]
                out[t, :, c * HEAD_DIM : (c + 1) * HEAD_DIM] = blocks[chunk][
                    pair * GROUPS + c // per_group,
                    (a * len(BACK[chunk]) + position) * SLOTS + slot,
                ]


def work_kernel(last, heads, before, place_ref, image_ref, gains_ref, blocks_ref, *refs):
    if before:
        before_ref, before_terms_ref = refs[:2]
    outs = refs[-len(BACK) :] if last else refs[-2:-1]
    where = chunk_of(BACK if last else (heads,))
    lengths = [len(chunk) for chunk in (BACK if last else (heads,))]
    shards = blocks_ref.shape[0]
    tile_count = image_ref.shape[1]
    rows = shards * SLOTS * PIECE_ROWS
    scale = 1.0 / math.sqrt(HEAD_DIM)
    f32, bf16 = jnp.float32, jnp.bfloat16
    _, long_count = packed_places(image_ref, tile_count)
    is_long = place_ref[0] // GROUPS < long_count

    period = SLOTS * PIECE_ROWS
    key_slot = lax.broadcasted_iota(jnp.int32, (period, rows), 0) // PIECE_ROWS % SLOTS
    query_slot = lax.broadcasted_iota(jnp.int32, (period, rows), 1) // PIECE_ROWS % SLOTS
    apart = jnp.where(is_long, 0.0, -1e30).astype(f32)
    bias = jnp.where(key_slot == query_slot, jnp.zeros((), f32), apart)

    def load(a, h):
        first = (a * len(heads) + heads.index(h)) * SLOTS
        return blocks_ref[:, first : first + SLOTS].astype(f32).reshape(rows, HEAD_DIM)

    def store(a, h, value):
        chunk, position = where[h]
        first = (a * lengths[chunk] + position) * SLOTS
        outs[chunk][:, first : first + SLOTS] = value.reshape(
            shards, SLOTS, PIECE_ROWS, HEAD_DIM
        ).astype(bf16)

    def normalize(raw, gain):
        inverse = lax.rsqrt(jnp.mean(raw * raw, axis=-1, keepdims=True) + epsilon)
        unit = raw * inverse
        return unit, inverse, (unit * gain).astype(bf16)

    def norm_back(grad_norm, unit, inverse, gain):
        grad = grad_norm.astype(bf16).astype(f32)
        direct = grad * gain
        inner = jnp.mean(direct * unit, axis=-1, keepdims=True)
        return inverse * (direct - unit * inner), jnp.sum(grad * unit, axis=0, keepdims=True)

    def dot(a, b, dims):
        return lax.dot_general(a, b, (dims, ((), ())), preferred_element_type=f32)

    query_gain = gains_ref[0:1, :]
    key_gain = gains_ref[1:2, :]
    query_term = jnp.zeros((1, HEAD_DIM), f32)
    key_term = jnp.zeros((1, HEAD_DIM), f32)
    for h in heads:
        query_unit, query_inverse, query_norm = normalize(load(0, h), query_gain)
        key_unit, key_inverse, key_norm = normalize(load(1, h), key_gain)
        value = load(2, h).astype(bf16)
        grad = load(3, h).astype(bf16)
        scores = dot(key_norm, query_norm, ((1,), (1,)))
        scores = (scores.reshape(shards, period, rows) + bias[None]).reshape(rows, rows)
        top = jnp.max(scores, axis=0, keepdims=True)
        powers = jnp.exp((scores - top) * scale)
        weights = powers * (1.0 / jnp.sum(powers, axis=0, keepdims=True))
        weight_grad = dot(value, grad, ((1,), (1,)))
        row_inner = jnp.sum(weights * weight_grad, axis=0, keepdims=True)
        score_grad = (weights * (weight_grad - row_inner)).astype(bf16)
        value_grad = dot(weights.astype(bf16), grad, ((1,), (0,)))
        key_norm_grad = dot(score_grad, query_norm, ((1,), (0,))) * scale
        query_norm_grad = dot(score_grad, key_norm, ((0,), (0,))) * scale
        query_grad, term = norm_back(query_norm_grad, query_unit, query_inverse, query_gain)
        query_term = query_term + term
        key_grad, term = norm_back(key_norm_grad, key_unit, key_inverse, key_gain)
        key_term = key_term + term
        store(0, h, query_grad)
        store(1, h, key_grad)
        store(2, h, value_grad)

    terms = jnp.concatenate([query_term, key_term], axis=0)
    if not last:
        refs[-1][...] = terms
        return
    if before:
        terms = terms + before_terms_ref[...]
        for a in range(3):
            for i, h in enumerate(before):
                chunk, position = where[h]
                first = (a * lengths[chunk] + position) * SLOTS
                held = (a * len(before) + i) * SLOTS
                outs[chunk][:, first : first + SLOTS] = before_ref[:, held : held + SLOTS]
    parts = []
    for _ in range(3):
        part = terms.astype(bf16).astype(f32)
        parts.append(part)
        terms = terms - part
    parts.append(jnp.zeros_like(terms))
    piece = jnp.concatenate(parts, axis=0).astype(bf16)
    end = outs[0].shape[1] - 1
    outs[0][:, end] = jnp.broadcast_to(piece[None], (shards,) + piece.shape)


SMEM = pl.BlockSpec(memory_space=pltpu.SMEM)
VMEM = pl.BlockSpec(memory_space=pltpu.VMEM)
HBM = pl.BlockSpec(memory_space=pltpu.HBM)


def params(mib):
    return pltpu.CompilerParams(vmem_limit_bytes=mib * 1024 * 1024)


def exchange(blocks):
    return lax.all_to_all(blocks, "ctx", split_axis=0, concat_axis=0, tiled=True)


def blocks(shards, pieces):
    return jax.ShapeDtypeStruct((shards, pieces, PIECE_ROWS, HEAD_DIM), jnp.bfloat16)


def there(chunks, queries, keys, values, out_grad, norm_gains, tile_image):
    shards = lax.axis_size("ctx")
    place = lax.axis_index("ctx").astype(jnp.int32).reshape(1)
    sources = (queries, keys, values, out_grad)
    packed = pl.pallas_call(
        functools.partial(pack_kernel, chunks),
        out_shape=[blocks(shards, 4 * len(chunk) * SLOTS) for chunk in chunks],
        in_specs=[HBM] * 5,
        out_specs=[VMEM] * len(chunks),
        scratch_shapes=[
            pltpu.SMEM(tile_image.shape, jnp.int32),
            pltpu.VMEM((4,) + queries.shape, jnp.bfloat16),
            pltpu.SemaphoreType.DMA(()),
            pltpu.SemaphoreType.DMA((4, 2)),
        ],
        compiler_params=params(62),
        name="pack",
    )(tile_image, *sources)
    before, worked = (), []
    arrived = []
    for chunk in packed:
        if arrived:
            arrived[-1], chunk = lax.optimization_barrier((arrived[-1], chunk))
        arrived.append(exchange(chunk))
    for heads, chunk in zip(chunks, arrived):
        last = heads is chunks[-1]
        if last:
            out_shape = [
                blocks(shards, 3 * len(chunk) * SLOTS + (i == 0)) for i, chunk in enumerate(BACK)
            ]
        else:
            out_shape = [
                blocks(shards, 3 * len(heads) * SLOTS),
                jax.ShapeDtypeStruct(norm_gains.shape, jnp.float32),
            ]
        worked = pl.pallas_call(
            functools.partial(work_kernel, last, heads, before),
            out_shape=out_shape,
            in_specs=[SMEM, SMEM, VMEM, VMEM] + [VMEM] * len(worked),
            out_specs=[VMEM] * len(out_shape),
            compiler_params=params(32),
            cost_estimate=pl.CostEstimate(
                flops=len(heads) * 10 * 512 * 512 * HEAD_DIM,
                bytes_accessed=len(heads) * 7 * 512 * HEAD_DIM * 2,
                transcendentals=len(heads) * 512 * 512,
            ),
            name="work",
        )(place, tile_image, norm_gains, chunk, *worked)
        before = before + heads
    return worked


def on_device(queries, keys, values, out_grad, norm_gains, tile_image):
    token_rows, width = queries.shape[1:]
    tile_count = tile_image.shape[1]
    tiled = (tile_count, PIECE_ROWS, width)
    early, late = lax.cond(
        lax.axis_index("dp") % 2 == 0,
        functools.partial(there, PLANS[0]),
        functools.partial(there, PLANS[1]),
        *[x.reshape(tiled) for x in (queries, keys, values, out_grad)],
        norm_gains,
        tile_image,
    )
    early_back = exchange(early)
    early_back, late = lax.optimization_barrier((early_back, late))
    late_back = exchange(late)
    last = early_back.shape[1] - 1
    pieces = jnp.sum(early_back[:, last, :6].astype(jnp.float32), axis=0)
    own_terms = jnp.sum(pieces.reshape(3, 2, HEAD_DIM), axis=0)
    gain_grad = jnp.sum(lax.all_gather(own_terms, "dp"), axis=0)

    grads = pl.pallas_call(
        unpack_kernel,
        out_shape=[jax.ShapeDtypeStruct(tiled, jnp.bfloat16)] * 3,
        in_specs=[SMEM, VMEM, VMEM],
        out_specs=[VMEM] * 3,
        compiler_params=params(16),
        name="unpack",
    )(tile_image, early_back, late_back)
    return (*[x.reshape(1, token_rows, width) for x in grads], gain_grad)


def solution(mesh):
    rows = P("dp", "ctx", None)
    in_specs = (rows, rows, rows, rows, P(), P("dp", None))
    out_specs = (rows, rows, rows, P())
    return jax.shard_map(
        on_device, mesh=mesh, in_specs=in_specs, out_specs=out_specs, check_vma=False
    )
```

time: 112 us -> 102 us (0.911)
  the two profiles are of different devices: /device:TPU:2 before, /device:TPU:1 now
where the time goes in v3:
time: 102 us; the launch traced here: 101 us
  blocking collectives  63.3 us (62%)
  waiting for transfers between devices  16.8 us (16%)
  Pallas kernels  10.5 us (10%)
  starting transfers between devices  9.17 us (9%)
    all_to_all x2, blocking collectives, exchange(): lax.all_to_all(blocks, 'ctx', split_axis=0, concat_axis=0, tiled=True)  47.3 us
    all_to_all x2, waiting for transfers between devices, exchange(): lax.all_to_all(blocks, 'ctx', split_axis=0, concat_axis=0, tiled=True)  16.8 us
    all_gather x1, blocking collectives, on_device(): gain_grad = jnp.sum(lax.all_gather(own_terms, 'dp'), axis=0)  16 us
    all_to_all x2, starting transfers between devices, exchange(): lax.all_to_all(blocks, 'ctx', split_axis=0, concat_axis=0, tiled=True)  9.17 us
    pallas_call x2, Pallas kernels, there(): pl.pallas_call(functools.partial(work_kernel, last, heads, before), out_s...  5.95 us
    pallas_call x1, Pallas kernels, there(): pl.pallas_call(functools.partial(pack_kernel, chunks), out_shape=[blocks(...  2.7 us
  transfers between devices with their start and end apart: 2, of which 2 were waited for; matrix products, arithmetic and copies ran while one was open for 1% of the time, Pallas kernels for 2%

profile of v3, /device:TPU:1, one launch (start us, length us, event | category | flops | bytes accessed | tf_op | source)
XLA Modules:
  0.0 101.2 jit_solution(10939023592528233867)
XLA Ops:
  0.6 60.1 %conditional.1 = ((bf16[32,7,8,128]{3,2,1,0:T(8,128)(2,1)S(1)}, bf16[32,12,8,128]{3,2,1,0:T(8,128)(2,1)})) conditional(s32[]{:T(128)} %convert_element_type.7, (s32[1,16]{1,0:T(1,128)}, bf16[16,8,1536]{2,1,0:T(8,128)(2,1)}, bf16[16,8,1536]{2,1,0:T(8,128)(2,1)}, bf16[16,8,1536]{2,1,0:T(8,128)(2,1)}, bf16[16,8,1536]{2,1,0:T(8,128)(2,1)}, ...), branch_computations={%region_0.1_spmd, %region_1.2_spmd} | conditional | flops 1006632960 | bytes 7475572 | solution.py:266
  0.7 2.7 %pack.2 = (bf16[32,8,8,128]{3,2,1,0:T(8,128)(2,1)}, bf16[32,16,8,128]{3,2,1,0:T(8,128)(2,1)}) custom-call(s32[1,16]{1,0:T(1,128)} %get-tuple-element.24.image_hbm.image_ref, bf16[16,8,1536]{2,1,0:T(8,128)(2,1)} %get-tuple-element.26.refs_0_, bf16[16,8,1536]{2,1,0:T(8,128)(2,1)} %get-tuple-element.27.refs_1_, bf16[16,8,1536]{2,1,0:T(8,128)(2,1)} %get-tuple-element.28.refs_2_, ...), custom_call_target="tpu_custom_call" | custom-call | tf_op jit(solution)/shard_map/cond/branch_0_fun/pack/pallas_call | solution.py:214
  3.4 0.0 copy-start.1
  3.4 0.0 copy-start.3
  3.4 30.4 %all_to_all.22.blocks_ref = bf16[32,8,8,128]{3,2,1,0:T(8,128)(2,1)S(1)} all-to-all(bf16[32,8,8,128]{3,2,1,0:T(8,128)(2,1)} %get-tuple-element.30), channel_id=1, replica_groups=mesh['dp'=16,'ctx'=32] {'ctx'}, dimensions={0} | all-to-all | bytes 1048576 | tf_op jit(solution)/shard_map/cond/branch_0_fun/all_to_all | solution.py:203
  33.8 5.2 %all-to-all-start.1 = ((bf16[32,16,8,128]{3,2,1,0:T(8,128)(2,1)}), bf16[32,16,8,128]{3,2,1,0:T(8,128)(2,1)S(1)}, u32[]{:S(2)}, u32[]{:S(2)}) async-start(bf16[32,16,8,128]{3,2,1,0:T(8,128)(2,1)} %get-tuple-element.32), calls=%async_computation.1 | async-start | bytes 2097152 | tf_op jit(solution)/shard_map/cond/branch_0_fun/all_to_all | solution.py:203
  39.0 0.0 copy-done.1
  39.0 0.0 copy-done.3
  39.1 2.0 %work.3 = (bf16[32,6,8,128]{3,2,1,0:T(8,128)(2,1)S(1)}, f32[2,128]{1,0:T(2,128)S(1)}) custom-call(s32[1]{0:T(128)} %bitcast.place_ref, s32[1,16]{1,0:T(1,128)S(1)} %copy-done.1, f32[2,128]{1,0:T(2,128)S(1)} %copy-done.3, bf16[32,8,8,128]{3,2,1,0:T(8,128)(2,1)S(1)} %all_to_all.22.blocks_ref), custom_call_target="tpu_custom_call" | custom-call | flops 335544320 | bytes 917504 | tf_op jit(solution)/shard_map/cond/branch_0_fun/work/pallas_call | solution.py:245
  41.1 15.7 %all-to-all-done.1.blocks_ref = bf16[32,16,8,128]{3,2,1,0:T(8,128)(2,1)S(1)} async-done(((bf16[32,16,8,128]{3,2,1,0:T(8,128)(2,1)}), bf16[32,16,8,128]{3,2,1,0:T(8,128)(2,1)S(1)}, u32[]{:S(2)}, u32[]{:S(2)}) %all-to-all-start.1) | async-done | bytes 1048608 | tf_op jit(solution)/shard_map/cond/branch_0_fun/all_to_all | solution.py:203
  56.8 3.9 %work.4 = (bf16[32,7,8,128]{3,2,1,0:T(8,128)(2,1)S(1)}, bf16[32,12,8,128]{3,2,1,0:T(8,128)(2,1)}) custom-call(s32[1]{0:T(128)} %bitcast.place_ref, s32[1,16]{1,0:T(1,128)S(1)} %copy-done.1, f32[2,128]{1,0:T(2,128)S(1)} %copy-done.3, bf16[32,16,8,128]{3,2,1,0:T(8,128)(2,1)S(1)} %all-to-all-done.1.blocks_ref, ...), custom_call_target="tpu_custom_call" | custom-call | flops 671088640 | bytes 1835008 | tf_op jit(solution)/shard_map/cond/branch_0_fun/work/pallas_call | solution.py:245
  60.7 0.0 copy-start
  60.7 16.9 %all_to_all.23.refs_0_ = bf16[32,7,8,128]{3,2,1,0:T(8,128)(2,1)S(1)} all-to-all(bf16[32,7,8,128]{3,2,1,0:T(8,128)(2,1)S(1)} %get-tuple-element.53), channel_id=1, replica_groups=mesh['dp'=16,'ctx'=32] {'ctx'}, dimensions={0} | all-to-all | bytes 917504 | tf_op jit(solution)/shard_map/all_to_all | solution.py:203
  77.6 3.9 %all-to-all-start.4 = ((bf16[32,12,8,128]{3,2,1,0:T(8,128)(2,1)}), bf16[32,12,8,128]{3,2,1,0:T(8,128)(2,1)S(1)}, u32[]{:S(2)}, u32[]{:S(2)}) async-start(bf16[32,12,8,128]{3,2,1,0:T(8,128)(2,1)} %get-tuple-element.56), calls=%async_computation.4 | async-start | bytes 1572864 | tf_op jit(solution)/shard_map/all_to_all | solution.py:203
  81.6 16.0 %all-gather.1 = f32[16,2,128]{2,1,0:T(2,128)S(1)} all-gather(f32[1,2,128]{2,1,0:T(2,128)S(1)} %bitcast.18), channel_id=2, replica_groups=mesh['dp'=16,'ctx'=32] {'dp'}, dimensions={0}, use_global_device_ids=true | all-gather | bytes 17408 | tf_op jit(solution)/shard_map/all_gather | solution.py:280
  97.6 0.6 reduce_sum.29
  98.2 1.1 %all-to-all-done.4.refs_1_ = bf16[32,12,8,128]{3,2,1,0:T(8,128)(2,1)S(1)} async-done(((bf16[32,12,8,128]{3,2,1,0:T(8,128)(2,1)}), bf16[32,12,8,128]{3,2,1,0:T(8,128)(2,1)S(1)}, u32[]{:S(2)}, u32[]{:S(2)}) %all-to-all-start.4) | async-done | bytes 786464 | tf_op jit(solution)/shard_map/all_to_all | solution.py:203
  99.4 0.0 copy-done
  99.4 1.9 %unpack.1 = (bf16[16,8,1536]{2,1,0:T(8,128)(2,1)}, bf16[16,8,1536]{2,1,0:T(8,128)(2,1)}, bf16[16,8,1536]{2,1,0:T(8,128)(2,1)}) custom-call(s32[1,16]{1,0:T(1,128)S(1)} %copy-done, bf16[32,7,8,128]{3,2,1,0:T(8,128)(2,1)S(1)} %all_to_all.23.refs_0_, bf16[32,12,8,128]{3,2,1,0:T(8,128)(2,1)S(1)} %all-to-all-done.4.refs_1_), custom_call_target="tpu_custom_call" | custom-call | tf_op jit(solution)/shard_map/unpack/pallas_call | solution.py:282
  (3 shorter events, 0.1 us)
Async XLA Ops:
  3.4 35.7 %copy-start.1 = (s32[1,16]{1,0:T(1,128)S(1)}, s32[1,16]{1,0:T(1,128)}, u32[]{:S(2)}) copy-start(s32[1,16]{1,0:T(1,128)} %get-tuple-element.24.image_hbm.image_ref) | copy-start | bytes 196 | tf_op jit(solution)/shard_map/cond
  3.4 35.7 %copy-start.3 = (f32[2,128]{1,0:T(2,128)S(1)}, f32[2,128]{1,0:T(2,128)}, u32[]{:S(2)}) copy-start(f32[2,128]{1,0:T(2,128)} %get-tuple-element.25.gains_ref) | copy-start | bytes 3076 | tf_op jit(solution)/shard_map/cond
  33.8 23.0 %all-to-all-start.1 = ((bf16[32,16,8,128]{3,2,1,0:T(8,128)(2,1)}), bf16[32,16,8,128]{3,2,1,0:T(8,128)(2,1)S(1)}, u32[]{:S(2)}, u32[]{:S(2)}) async-start(bf16[32,16,8,128]{3,2,1,0:T(8,128)(2,1)} %get-tuple-element.32), calls=%async_computation.1 | async-start | bytes 2097152 | tf_op jit(solution)/shard_map/cond/branch_0_fun/all_to_all | solution.py:203
  60.7 38.7 %copy-start = (s32[1,16]{1,0:T(1,128)S(1)}, s32[1,16]{1,0:T(1,128)}, u32[]{:S(2)}) copy-start(s32[1,16]{1,0:T(1,128)} %image_ref.1) | copy-start | bytes 196
  77.6 21.8 %all-to-all-start.4 = ((bf16[32,12,8,128]{3,2,1,0:T(8,128)(2,1)}), bf16[32,12,8,128]{3,2,1,0:T(8,128)(2,1)S(1)}, u32[]{:S(2)}, u32[]{:S(2)}) async-start(bf16[32,12,8,128]{3,2,1,0:T(8,128)(2,1)} %get-tuple-element.56), calls=%async_computation.4 | async-start | bytes 1572864 | tf_op jit(solution)/shard_map/all_to_all | solution.py:203

commit v4 on v3

v4 whole, which is shorter than its diff:
```python
import functools
import math

import jax
import jax.numpy as jnp
from jax import lax
from jax.experimental import pallas as pl
from jax.experimental.pallas import tpu as pltpu
from jax.sharding import PartitionSpec as P

epsilon = 1e-06

GROUPS = 4
PER_GROUP = 3
SLOTS = 2
PIECE_ROWS = 8
HEAD_DIM = 128

PLANS = (((0, 1, 2),), ((0,), (1, 2)))
BACK = ((2,), (0, 1))


def located(chunks, arrays):
    return {
        (a, h): (i, (a * len(chunk) + n) * SLOTS)
        for i, chunk in enumerate(chunks)
        for a in range(arrays)
        for n, h in enumerate(chunk)
    }


def packed_places(image_ref, tile_count):
    images = [image_ref[0, t] for t in range(tile_count)]
    one = jnp.int32(1)
    zero = jnp.int32(0)
    joined = [zero] + [
        jnp.where(images[t] == images[t - 1], one, zero) for t in range(1, tile_count)
    ]
    long_count = sum(joined[1:], zero)
    long_next = zero
    short_next = long_count * 2
    places = []
    for t in range(tile_count):
        ahead = joined[t + 1] if t + 1 < tile_count else zero
        in_long = joined[t] + ahead
        places.append(jnp.where(in_long > 0, long_next, short_next))
        long_next = long_next + in_long
        short_next = short_next + (1 - in_long)
    return places, long_count


def pack_kernel(chunks, image_hbm, *refs):
    sources, outs = refs[:4], refs[4 : 4 + len(chunks)]
    image_ref, held, image_sem, in_sems, out_sems, *packed = refs[4 + len(chunks) :]
    tile_count = held.shape[1]
    heads = held.shape[3] // HEAD_DIM
    half = tile_count // 2
    where = located(chunks, 4)
    image_copy = pltpu.make_async_copy(image_hbm, image_ref, image_sem)
    image_copy.start()
    arriving = []
    for a, source in enumerate(sources):
        for part in range(2):
            tiles = pl.ds(part * half, half)
            copy = pltpu.make_async_copy(source.at[tiles], held.at[a, tiles], in_sems.at[a, part])
            copy.start()
            arriving.append(copy)
    image_copy.wait()
    places, _ = packed_places(image_ref, tile_count)
    leaving = []
    for a in range(len(sources)):
        for t in range(tile_count):
            if t % half == 0:
                arriving[a * 2 + t // half].wait()
            pair = places[t] // SLOTS
            slot = places[t] % SLOTS
            for c in range(heads):
                chunk, piece = where[a, c % PER_GROUP]
                packed[chunk][pair * GROUPS + c // PER_GROUP, piece + slot] = held[
                    a, t, :, c * HEAD_DIM : (c + 1) * HEAD_DIM
                ]
        for i, chunk in enumerate(chunks):
            pieces = pl.ds(a * len(chunk) * SLOTS, len(chunk) * SLOTS)
            copy = pltpu.make_async_copy(
                packed[i].at[:, pieces], outs[i].at[:, pieces], out_sems.at[i, a]
            )
            copy.start()
            leaving.append(copy)
    for copy in leaving:
        copy.wait()


def unpack_kernel(image_ref, terms_ref, *refs):
    blocks = refs[: len(BACK)]
    *outs, gain_hbm, held, gain_ref, sems = refs[len(BACK) :]
    tile_count = held.shape[1]
    heads = held.shape[3] // HEAD_DIM
    where = located(BACK, len(outs))
    gain_ref[...] = jnp.sum(terms_ref[...], axis=0)
    leaving = [pltpu.make_async_copy(gain_ref, gain_hbm, sems.at[len(outs)])]
    leaving[0].start()
    places, _ = packed_places(image_ref, tile_count)
    for a, out in enumerate(outs):
        for t in range(tile_count):
            pair = places[t] // SLOTS
            slot = places[t] % SLOTS
            for c in range(heads):
                chunk, piece = where[a, c % PER_GROUP]
                held[a, t, :, c * HEAD_DIM : (c + 1) * HEAD_DIM] = blocks[chunk][
                    pair * GROUPS + c // PER_GROUP, piece + slot
                ]
        copy = pltpu.make_async_copy(held.at[a], out, sems.at[a])
        copy.start()
        leaving.append(copy)
    for copy in leaving:
        copy.wait()


def work_kernel(heads, before, long_ref, gains_ref, blocks_ref, *refs):
    last = heads[-1] == PER_GROUP - 1
    if before:
        before_ref, before_terms_ref = refs[:2]
        refs = refs[2:]
    if last:
        early_ref, late_hbm, late_ref, sems = refs
        goes_to = located(BACK, 3)
    else:
        early_ref, terms_ref = refs
        goes_to = located((heads,), 3)
    arrived_at = located((heads,), 4)
    shards = blocks_ref.shape[0]
    leaving = []

    def leave(source, piece):
        pieces = pl.ds(piece, SLOTS)
        copy = pltpu.make_async_copy(source, late_hbm.at[:, pieces], sems.at[piece // SLOTS])
        copy.start()
        leaving.append(copy)

    for (a, h), (_, piece) in located((before,), 3).items():
        leave(before_ref.at[:, pl.ds(piece, SLOTS)], goes_to[a, h][1])
    rows = shards * SLOTS * PIECE_ROWS
    scale = 1.0 / math.sqrt(HEAD_DIM)
    f32, bf16 = jnp.float32, jnp.bfloat16
    is_long = long_ref[0] > 0

    period = SLOTS * PIECE_ROWS
    key_slot = lax.broadcasted_iota(jnp.int32, (period, rows), 0) // PIECE_ROWS % SLOTS
    query_slot = lax.broadcasted_iota(jnp.int32, (period, rows), 1) // PIECE_ROWS % SLOTS
    apart = jnp.where(is_long, 0.0, -1e30).astype(f32)
    bias = jnp.where(key_slot == query_slot, jnp.zeros((), f32), apart)

    def load(a, h):
        piece = arrived_at[a, h][1]
        return blocks_ref[:, piece : piece + SLOTS].astype(f32).reshape(rows, HEAD_DIM)

    def store(a, h, value):
        chunk, piece = goes_to[a, h]
        held = late_ref if chunk else early_ref
        held[:, piece : piece + SLOTS] = value.reshape(
            shards, SLOTS, PIECE_ROWS, HEAD_DIM
        ).astype(bf16)
        if chunk:
            leave(late_ref.at[:, pl.ds(piece, SLOTS)], piece)

    def normalize(raw, gain):
        inverse = lax.rsqrt(jnp.mean(raw * raw, axis=-1, keepdims=True) + epsilon)
        unit = raw * inverse
        return unit, inverse, (unit * gain).astype(bf16)

    def norm_back(grad_norm, unit, inverse, gain):
        grad = grad_norm.astype(bf16).astype(f32)
        direct = grad * gain
        inner = jnp.mean(direct * unit, axis=-1, keepdims=True)
        return inverse * (direct - unit * inner), jnp.sum(grad * unit, axis=0, keepdims=True)

    def dot(a, b, dims):
        return lax.dot_general(a, b, (dims, ((), ())), preferred_element_type=f32)

    query_gain = gains_ref[0:1, :]
    key_gain = gains_ref[1:2, :]
    query_term = jnp.zeros((1, HEAD_DIM), f32)
    key_term = jnp.zeros((1, HEAD_DIM), f32)
    for h in heads:
        query_unit, query_inverse, query_norm = normalize(load(0, h), query_gain)
        key_unit, key_inverse, key_norm = normalize(load(1, h), key_gain)
        value = load(2, h).astype(bf16)
        grad = load(3, h).astype(bf16)
        scores = dot(key_norm, query_norm, ((1,), (1,)))
        scores = (scores.reshape(shards, period, rows) + bias[None]).reshape(rows, rows)
        top = jnp.max(scores, axis=0, keepdims=True)
        powers = jnp.exp2((scores - top) * (scale * math.log2(math.e)))
        weights = powers * (1.0 / jnp.sum(powers, axis=0, keepdims=True))
        weight_grad = dot(value, grad, ((1,), (1,)))
        row_inner = jnp.sum(weights * weight_grad, axis=0, keepdims=True)
        score_grad = (weights * (weight_grad - row_inner)).astype(bf16)
        value_grad = dot(weights.astype(bf16), grad, ((1,), (0,)))
        key_norm_grad = dot(score_grad, query_norm, ((1,), (0,))) * scale
        query_norm_grad = dot(score_grad, key_norm, ((0,), (0,))) * scale
        query_grad, term = norm_back(query_norm_grad, query_unit, query_inverse, query_gain)
        query_term = query_term + term
        key_grad, term = norm_back(key_norm_grad, key_unit, key_inverse, key_gain)
        key_term = key_term + term
        store(0, h, query_grad)
        store(1, h, key_grad)
        store(2, h, value_grad)

    terms = jnp.concatenate([query_term, key_term], axis=0)
    if not last:
        terms_ref[...] = terms
        return
    if before:
        terms = terms + before_terms_ref[...]
    parts = []
    for _ in range(3):
        part = terms.astype(bf16).astype(f32)
        parts.append(part)
        terms = terms - part
    parts.append(jnp.zeros_like(terms))
    piece = jnp.concatenate(parts, axis=0).astype(bf16)
    early_ref[:, early_ref.shape[1] - 1] = jnp.broadcast_to(piece[None], (shards,) + piece.shape)
    for copy in leaving:
        copy.wait()


SMEM = pl.BlockSpec(memory_space=pltpu.SMEM)
VMEM = pl.BlockSpec(memory_space=pltpu.VMEM)
HBM = pl.BlockSpec(memory_space=pltpu.HBM)


def params(mib):
    return pltpu.CompilerParams(vmem_limit_bytes=mib * 1024 * 1024)


def exchange(blocks):
    return lax.all_to_all(blocks, "ctx", split_axis=0, concat_axis=0, tiled=True)


def block_shape(shards, pairs, extra=0):
    return (shards, pairs * SLOTS + extra, PIECE_ROWS, HEAD_DIM)


def there(chunks, queries, keys, values, out_grad, norm_gains, tile_image):
    bf16, f32 = jnp.bfloat16, jnp.float32
    shards = lax.axis_size("ctx")
    place = lax.axis_index("ctx").astype(jnp.int32).reshape(1)
    shapes = [block_shape(shards, 4 * len(chunk)) for chunk in chunks]
    packed = pl.pallas_call(
        functools.partial(pack_kernel, chunks),
        out_shape=[jax.ShapeDtypeStruct(shape, bf16) for shape in shapes],
        in_specs=[HBM] * 5,
        out_specs=[HBM] * len(chunks),
        scratch_shapes=[
            pltpu.SMEM(tile_image.shape, jnp.int32),
            pltpu.VMEM((4,) + queries.shape, bf16),
            pltpu.SemaphoreType.DMA(()),
            pltpu.SemaphoreType.DMA((4, 2)),
            pltpu.SemaphoreType.DMA((len(chunks), 4)),
        ]
        + [pltpu.VMEM(shape, bf16) for shape in shapes],
        compiler_params=params(62),
        name="pack",
    )(tile_image, queries, keys, values, out_grad)
    *packed, tile_image = lax.optimization_barrier((*packed, tile_image))
    long_count = jnp.sum((tile_image[0, 1:] == tile_image[0, :-1]).astype(jnp.int32))
    is_long = (place // GROUPS < long_count).astype(jnp.int32)

    arrived = []
    for chunk in packed:
        if arrived:
            arrived[-1], chunk = lax.optimization_barrier((arrived[-1], chunk))
        arrived.append(exchange(chunk))

    before, worked = (), ()
    for heads, chunk in zip(chunks, arrived):
        if heads is chunks[-1]:
            early_shape, late_shape = (
                block_shape(shards, 3 * len(back), int(i == 0)) for i, back in enumerate(BACK)
            )
            out_shape = [
                jax.ShapeDtypeStruct(early_shape, bf16),
                jax.ShapeDtypeStruct(late_shape, bf16),
            ]
            out_specs = [VMEM, HBM]
            scratch_shapes = [
                pltpu.VMEM(late_shape, bf16),
                pltpu.SemaphoreType.DMA((3 * len(BACK[1]),)),
            ]
        else:
            out_shape = [
                jax.ShapeDtypeStruct(block_shape(shards, 3 * len(heads)), bf16),
                jax.ShapeDtypeStruct(norm_gains.shape, f32),
            ]
            out_specs = [VMEM, VMEM]
            scratch_shapes = []
        worked = pl.pallas_call(
            functools.partial(work_kernel, heads, before),
            out_shape=out_shape,
            in_specs=[SMEM, VMEM, VMEM] + [VMEM] * len(worked),
            out_specs=out_specs,
            scratch_shapes=scratch_shapes,
            compiler_params=params(32),
            cost_estimate=pl.CostEstimate(
                flops=len(heads) * 10 * 512 * 512 * HEAD_DIM,
                bytes_accessed=len(heads) * 7 * 512 * HEAD_DIM * 2,
                transcendentals=len(heads) * 512 * 512,
            ),
            name="work",
        )(is_long, norm_gains, chunk, *worked)
        before = before + heads
    return worked


def on_device(queries, keys, values, out_grad, norm_gains, tile_image):
    token_rows, width = queries.shape[1:]
    tile_count = tile_image.shape[1]
    tiled = (tile_count, PIECE_ROWS, width)
    early, late = lax.cond(
        lax.axis_index("dp") % 2 == 0,
        functools.partial(there, PLANS[0]),
        functools.partial(there, PLANS[1]),
        *[x.reshape(tiled) for x in (queries, keys, values, out_grad)],
        norm_gains,
        tile_image,
    )
    early_back = exchange(early)
    early_back, late = lax.optimization_barrier((early_back, late))
    late_back = exchange(late)
    last = early_back.shape[1] - 1
    pieces = jnp.sum(early_back[:, last, :6].astype(jnp.float32), axis=0)
    own_terms = jnp.sum(pieces.reshape(3, 2, HEAD_DIM), axis=0)
    all_terms = lax.all_gather(own_terms, "dp")

    *grads, gain_grad = pl.pallas_call(
        unpack_kernel,
        out_shape=[jax.ShapeDtypeStruct(tiled, jnp.bfloat16)] * 3
        + [jax.ShapeDtypeStruct(norm_gains.shape, jnp.float32)],
        in_specs=[SMEM, VMEM, VMEM, VMEM],
        out_specs=[HBM] * 4,
        scratch_shapes=[
            pltpu.VMEM((3,) + tiled, jnp.bfloat16),
            pltpu.VMEM(norm_gains.shape, jnp.float32),
            pltpu.SemaphoreType.DMA((4,)),
        ],
        compiler_params=params(16),
        name="unpack",
    )(tile_image, all_terms, early_back, late_back)
    return (*[x.reshape(1, token_rows, width) for x in grads], gain_grad)


def solution(mesh):
    rows = P("dp", "ctx", None)
    in_specs = (rows, rows, rows, rows, P(), P("dp", None))
    out_specs = (rows, rows, rows, P())
    return jax.shard_map(
        on_device, mesh=mesh, in_specs=in_specs, out_specs=out_specs, check_vma=False
    )
```

time: 102 us -> 100 us (0.980)
  Pallas kernels: 10.5 us -> 8.76 us
    pallas_call x3, Pallas kernels: 8.65 us -> 6.92 us  [the longest x2 4.44 us: there(): pl.pallas_call(functools.partial(work_kernel, heads, before), out_shape=o...]
  transfers between devices with their start and end apart: 2 -> 2, of which waited for: 2 -> 2; matrix products, arithmetic and copies ran while one was open for 1% -> 1% of each run, Pallas kernels for 2% -> 1%
where the time goes in v4:
time: 100 us; the launch traced here: 99.8 us
  blocking collectives  63.4 us (63%)
  waiting for transfers between devices  16.3 us (16%)
  starting transfers between devices  9.21 us (9%)
  Pallas kernels  8.76 us (9%)
    all_to_all x2, blocking collectives, exchange(): lax.all_to_all(blocks, 'ctx', split_axis=0, concat_axis=0, tiled=True)  47.3 us
    all_to_all x2, waiting for transfers between devices, exchange(): lax.all_to_all(blocks, 'ctx', split_axis=0, concat_axis=0, tiled=True)  16.3 us
    all_gather x1, blocking collectives, on_device(): all_terms = lax.all_gather(own_terms, 'dp')  16 us
    all_to_all x2, starting transfers between devices, exchange(): lax.all_to_all(blocks, 'ctx', split_axis=0, concat_axis=0, tiled=True)  9.21 us
    pallas_call x2, Pallas kernels, there(): pl.pallas_call(functools.partial(work_kernel, heads, before), out_shape=o...  4.44 us
    pallas_call x1, Pallas kernels, there(): pl.pallas_call(functools.partial(pack_kernel, chunks), out_shape=[jax.Sha...  2.48 us
  transfers between devices with their start and end apart: 2, of which 2 were waited for; matrix products, arithmetic and copies ran while one was open for 1% of the time, Pallas kernels for 1%

profile of v4, /device:TPU:1, one launch (start us, length us, event | category | flops | bytes accessed | tf_op | source)
XLA Modules:
  0.0 99.8 jit_solution(4619460985949506001)
XLA Ops:
  0.6 58.8 %conditional.1 = ((bf16[32,7,8,128]{3,2,1,0:T(8,128)(2,1)S(1)}, bf16[32,12,8,128]{3,2,1,0:T(8,128)(2,1)})) conditional(s32[]{:T(128)} %convert_element_type.21, (s32[1,16]{1,0:T(1,128)}, bf16[16,8,1536]{2,1,0:T(8,128)(2,1)}, bf16[16,8,1536]{2,1,0:T(8,128)(2,1)}, bf16[16,8,1536]{2,1,0:T(8,128)(2,1)}, bf16[16,8,1536]{2,1,0:T(8,128)(2,1)}, ...), branch_computations={%region_0.2_spmd, %region_2.4_spmd} | conditional | flops 1006633024 | bytes 7475860 | solution.py:318
  0.7 2.5 %pack.2 = (bf16[32,8,8,128]{3,2,1,0:T(8,128)(2,1)}, bf16[32,16,8,128]{3,2,1,0:T(8,128)(2,1)}) custom-call(s32[1,16]{1,0:T(1,128)} %get-tuple-element.31.image_hbm, bf16[16,8,1536]{2,1,0:T(8,128)(2,1)} %get-tuple-element.25.refs_0_, bf16[16,8,1536]{2,1,0:T(8,128)(2,1)} %get-tuple-element.26.refs_1_, bf16[16,8,1536]{2,1,0:T(8,128)(2,1)} %get-tuple-element.27.refs_2_, ...), custom_call_target="tpu_custom_call" | custom-call | tf_op jit(solution)/shard_map/cond/branch_0_fun/pack/pallas_call | solution.py:248
  3.1 0.0 copy-start.1
  3.2 0.0 copy-start.3
  3.2 30.5 %all_to_all.22.blocks_ref = bf16[32,8,8,128]{3,2,1,0:T(8,128)(2,1)S(1)} all-to-all(bf16[32,8,8,128]{3,2,1,0:T(8,128)(2,1)} %get-tuple-element.33), channel_id=1, replica_groups=mesh['dp'=16,'ctx'=32] {'ctx'}, dimensions={0} | all-to-all | bytes 1048576 | tf_op jit(solution)/shard_map/cond/branch_0_fun/all_to_all | solution.py:236
  33.6 5.3 %all-to-all-start.1 = ((bf16[32,16,8,128]{3,2,1,0:T(8,128)(2,1)}), bf16[32,16,8,128]{3,2,1,0:T(8,128)(2,1)S(1)}, u32[]{:S(2)}, u32[]{:S(2)}) async-start(bf16[32,16,8,128]{3,2,1,0:T(8,128)(2,1)} %get-tuple-element.35), calls=%async_computation.1 | async-start | bytes 2097152 | tf_op jit(solution)/shard_map/cond/branch_0_fun/all_to_all | solution.py:236
  38.9 0.0 copy-done.1
  38.9 0.7 fusion
  40.3 0.0 copy-done.3
  40.3 1.5 %work.3 = (bf16[32,6,8,128]{3,2,1,0:T(8,128)(2,1)S(1)}, f32[2,128]{1,0:T(2,128)S(1)}) custom-call(s32[1]{0:T(128)S(6)} %convert_element_type.16.long_ref, f32[2,128]{1,0:T(2,128)S(1)} %copy-done.3, bf16[32,8,8,128]{3,2,1,0:T(8,128)(2,1)S(1)} %all_to_all.22.blocks_ref), custom_call_target="tpu_custom_call" | custom-call | flops 335544320 | bytes 917504 | tf_op jit(solution)/shard_map/cond/branch_0_fun/work/pallas_call | solution.py:296
  41.8 14.7 %all-to-all-done.1.blocks_ref = bf16[32,16,8,128]{3,2,1,0:T(8,128)(2,1)S(1)} async-done(((bf16[32,16,8,128]{3,2,1,0:T(8,128)(2,1)}), bf16[32,16,8,128]{3,2,1,0:T(8,128)(2,1)S(1)}, u32[]{:S(2)}, u32[]{:S(2)}) %all-to-all-start.1) | async-done | bytes 1048608 | tf_op jit(solution)/shard_map/cond/branch_0_fun/all_to_all | solution.py:236
  56.5 3.0 %work.4 = (bf16[32,7,8,128]{3,2,1,0:T(8,128)(2,1)S(1)}, bf16[32,12,8,128]{3,2,1,0:T(8,128)(2,1)}) custom-call(s32[1]{0:T(128)S(6)} %convert_element_type.16.long_ref, f32[2,128]{1,0:T(2,128)S(1)} %copy-done.3, bf16[32,16,8,128]{3,2,1,0:T(8,128)(2,1)S(1)} %all-to-all-done.1.blocks_ref, bf16[32,6,8,128]{3,2,1,0:T(8,128)(2,1)S(1)} %get-tuple-element.37.refs_0_, ...), custom_call_target="tpu_custom_call" | custom-call | flops 671088640 | bytes 1835008 | tf_op jit(solution)/shard_map/cond/branch_0_fun/work/pallas_call | solution.py:296
  59.5 0.0 copy-start
  59.5 16.9 %all_to_all.23.refs_0_ = bf16[32,7,8,128]{3,2,1,0:T(8,128)(2,1)S(1)} all-to-all(bf16[32,7,8,128]{3,2,1,0:T(8,128)(2,1)S(1)} %get-tuple-element.59), channel_id=1, replica_groups=mesh['dp'=16,'ctx'=32] {'ctx'}, dimensions={0} | all-to-all | bytes 917504 | tf_op jit(solution)/shard_map/all_to_all | solution.py:236
  76.4 3.9 %all-to-all-start.4 = ((bf16[32,12,8,128]{3,2,1,0:T(8,128)(2,1)}), bf16[32,12,8,128]{3,2,1,0:T(8,128)(2,1)S(1)}, u32[]{:S(2)}, u32[]{:S(2)}) async-start(bf16[32,12,8,128]{3,2,1,0:T(8,128)(2,1)} %get-tuple-element.62), calls=%async_computation.4 | async-start | bytes 1572864 | tf_op jit(solution)/shard_map/all_to_all | solution.py:236
  80.4 16.0 %all-gather.1.terms_ref = f32[16,2,128]{2,1,0:T(2,128)S(1)} all-gather(f32[1,2,128]{2,1,0:T(2,128)S(1)} %bitcast.20), channel_id=2, replica_groups=mesh['dp'=16,'ctx'=32] {'dp'}, dimensions={0}, use_global_device_ids=true | all-gather | bytes 17408 | tf_op jit(solution)/shard_map/all_gather | solution.py:332
  96.4 1.5 %all-to-all-done.4.refs_1_ = bf16[32,12,8,128]{3,2,1,0:T(8,128)(2,1)S(1)} async-done(((bf16[32,12,8,128]{3,2,1,0:T(8,128)(2,1)}), bf16[32,12,8,128]{3,2,1,0:T(8,128)(2,1)S(1)}, u32[]{:S(2)}, u32[]{:S(2)}) %all-to-all-start.4) | async-done | bytes 786464 | tf_op jit(solution)/shard_map/all_to_all | solution.py:236
  98.0 0.0 copy-done
  98.0 1.8 %unpack.1 = (bf16[16,8,1536]{2,1,0:T(8,128)(2,1)}, bf16[16,8,1536]{2,1,0:T(8,128)(2,1)}, bf16[16,8,1536]{2,1,0:T(8,128)(2,1)}, f32[2,128]{1,0:T(2,128)}) custom-call(s32[1,16]{1,0:T(1,128)S(1)} %copy-done, f32[16,2,128]{2,1,0:T(2,128)S(1)} %all-gather.1.terms_ref, bf16[32,7,8,128]{3,2,1,0:T(8,128)(2,1)S(1)} %all_to_all.23.refs_0_, ...), custom_call_target="tpu_custom_call" | custom-call | tf_op jit(solution)/shard_map/unpack/pallas_call | solution.py:334
  (3 shorter events, 0.1 us)
Async XLA Ops:
  3.1 35.8 %copy-start.1 = (s32[1,16]{1,0:T(1,128)S(1)}, s32[1,16]{1,0:T(1,128)}, u32[]{:S(2)}) copy-start(s32[1,16]{1,0:T(1,128)} %get-tuple-element.31.image_hbm) | copy-start | bytes 196 | tf_op jit(solution)/shard_map/cond
  3.2 37.1 %copy-start.3 = (f32[2,128]{1,0:T(2,128)S(1)}, f32[2,128]{1,0:T(2,128)}, u32[]{:S(2)}) copy-start(f32[2,128]{1,0:T(2,128)} %get-tuple-element.32.gains_ref) | copy-start | bytes 3076 | tf_op jit(solution)/shard_map/cond
  33.6 22.9 %all-to-all-start.1 = ((bf16[32,16,8,128]{3,2,1,0:T(8,128)(2,1)}), bf16[32,16,8,128]{3,2,1,0:T(8,128)(2,1)S(1)}, u32[]{:S(2)}, u32[]{:S(2)}) async-start(bf16[32,16,8,128]{3,2,1,0:T(8,128)(2,1)} %get-tuple-element.35), calls=%async_computation.1 | async-start | bytes 2097152 | tf_op jit(solution)/shard_map/cond/branch_0_fun/all_to_all | solution.py:236
  59.5 38.5 %copy-start = (s32[1,16]{1,0:T(1,128)S(1)}, s32[1,16]{1,0:T(1,128)}, u32[]{:S(2)}) copy-start(s32[1,16]{1,0:T(1,128)} %image_ref.1) | copy-start | bytes 196
  76.4 21.6 %all-to-all-start.4 = ((bf16[32,12,8,128]{3,2,1,0:T(8,128)(2,1)}), bf16[32,12,8,128]{3,2,1,0:T(8,128)(2,1)S(1)}, u32[]{:S(2)}, u32[]{:S(2)}) async-start(bf16[32,12,8,128]{3,2,1,0:T(8,128)(2,1)} %get-tuple-element.62), calls=%async_computation.4 | async-start | bytes 1572864 | tf_op jit(solution)/shard_map/all_to_all | solution.py:236

commit v5 on v4

--- a/solution.py
+++ b/solution.py
@@ -49,43 +49,43 @@
     return places, long_count
 
 
-def pack_kernel(chunks, image_hbm, *refs):
-    sources, outs = refs[:4], refs[4 : 4 + len(chunks)]
-    image_ref, held, image_sem, in_sems, out_sems, *packed = refs[4 + len(chunks) :]
-    tile_count = held.shape[1]
-    heads = held.shape[3] // HEAD_DIM
-    half = tile_count // 2
-    where = located(chunks, 4)
+def pack_kernel(heads, image_hbm, *refs):
+    *sources, out_hbm, image_ref, held, packed, image_sem, in_sems, out_sems = refs
+    arrays, tile_count = held.shape[:2]
+    taken = len(heads) * HEAD_DIM
     image_copy = pltpu.make_async_copy(image_hbm, image_ref, image_sem)
     image_copy.start()
     arriving = []
     for a, source in enumerate(sources):
-        for part in range(2):
-            tiles = pl.ds(part * half, half)
-            copy = pltpu.make_async_copy(source.at[tiles], held.at[a, tiles], in_sems.at[a, part])
+        for g in range(GROUPS):
+            columns = pl.ds((g * PER_GROUP + heads[0]) * HEAD_DIM, taken)
+            copy = pltpu.make_async_copy(
+                source.at[:, :, columns],
+                held.at[a, :, :, pl.ds(g * taken, taken)],
+                in_sems.at[a, g],
+            )
             copy.start()
             arriving.append(copy)
     image_copy.wait()
     places, _ = packed_places(image_ref, tile_count)
     leaving = []
-    for a in range(len(sources)):
-        for t in range(tile_count):
-            if t % half == 0:
-                arriving[a * 2 + t // half].wait()
-            pair = places[t] // SLOTS
-            slot = places[t] % SLOTS
-            for c in range(heads):
-                chunk, piece = where[a, c % PER_GROUP]
-                packed[chunk][pair * GROUPS + c // PER_GROUP, piece + slot] = held[
-                    a, t, :, c * HEAD_DIM : (c + 1) * HEAD_DIM
-                ]
-        for i, chunk in enumerate(chunks):
-            pieces = pl.ds(a * len(chunk) * SLOTS, len(chunk) * SLOTS)
-            copy = pltpu.make_async_copy(
-                packed[i].at[:, pieces], outs[i].at[:, pieces], out_sems.at[i, a]
-            )
-            copy.start()
-            leaving.append(copy)
+    for a in range(arrays):
+        for g in range(GROUPS):
+            arriving[a * GROUPS + g].wait()
+            for t in range(tile_count):
+                pair = places[t] // SLOTS
+                slot = places[t] % SLOTS
+                for n in range(len(heads)):
+                    first = (g * len(heads) + n) * HEAD_DIM
+                    packed[pair * GROUPS + g, (a * len(heads) + n) * SLOTS + slot] = held[
+                        a, t, :, first : first + HEAD_DIM
+                    ]
+        pieces = pl.ds(a * len(heads) * SLOTS, len(heads) * SLOTS)
+        copy = pltpu.make_async_copy(
+            packed.at[:, pieces], out_hbm.at[:, pieces], out_sems.at[a]
+        )
+        copy.start()
+        leaving.append(copy)
     for copy in leaving:
         copy.wait()
 
@@ -244,24 +244,34 @@
     bf16, f32 = jnp.bfloat16, jnp.float32
     shards = lax.axis_size("ctx")
     place = lax.axis_index("ctx").astype(jnp.int32).reshape(1)
-    shapes = [block_shape(shards, 4 * len(chunk)) for chunk in chunks]
-    packed = pl.pallas_call(
-        functools.partial(pack_kernel, chunks),
-        out_shape=[jax.ShapeDtypeStruct(shape, bf16) for shape in shapes],
-        in_specs=[HBM] * 5,
-        out_specs=[HBM] * len(chunks),
-        scratch_shapes=[
-            pltpu.SMEM(tile_image.shape, jnp.int32),
-            pltpu.VMEM((4,) + queries.shape, bf16),
-            pltpu.SemaphoreType.DMA(()),
-            pltpu.SemaphoreType.DMA((4, 2)),
-            pltpu.SemaphoreType.DMA((len(chunks), 4)),
-        ]
-        + [pltpu.VMEM(shape, bf16) for shape in shapes],
-        compiler_params=params(62),
-        name="pack",
-    )(tile_image, queries, keys, values, out_grad)
-    *packed, tile_image = lax.optimization_barrier((*packed, tile_image))
+    sources = (queries, keys, values, out_grad)
+    tile_count = queries.shape[0]
+    packed = []
+    for heads in chunks:
+        shape = block_shape(shards, 4 * len(heads))
+        taken = (4, tile_count, PIECE_ROWS, GROUPS * len(heads) * HEAD_DIM)
+        packed.append(
+            pl.pallas_call(
+                functools.partial(pack_kernel, heads),
+                out_shape=jax.ShapeDtypeStruct(shape, bf16),
+                in_specs=[HBM] * 5,
+                out_specs=HBM,
+                scratch_shapes=[
+                    pltpu.SMEM(tile_image.shape, jnp.int32),
+                    pltpu.VMEM(taken, bf16),
+                    pltpu.VMEM(shape, bf16),
+                    pltpu.SemaphoreType.DMA(()),
+                    pltpu.SemaphoreType.DMA((4, GROUPS)),
+                    pltpu.SemaphoreType.DMA((4,)),
+                ],
+                compiler_params=params(62),
+                cost_estimate=pl.CostEstimate(
+                    flops=0, bytes_accessed=16 * math.prod(shape), transcendentals=0
+                ),
+                name="pack",
+            )(tile_image, *sources)
+        )
+    packed[0], tile_image = lax.optimization_barrier((packed[0], tile_image))
     long_count = jnp.sum((tile_image[0, 1:] == tile_image[0, :-1]).astype(jnp.int32))
     is_long = (place // GROUPS < long_count).astype(jnp.int32)
 

time: 100 us -> 100 us (level)
  blocking collectives: 63.4 us -> 32.7 us
  waiting for transfers between devices: 16.3 us -> 30.8 us
  starting transfers between devices: 9.21 us -> 23.4 us
  Pallas kernels: 8.76 us -> 10.3 us
    all_to_all x2 -> x1, blocking collectives: 47.3 us -> 16.7 us  [exchange(): lax.all_to_all(blocks, 'ctx', split_axis=0, concat_axis=0, tiled=True)]
    all_to_all x2 -> x3, waiting for transfers between devices: 16.3 us -> 30.8 us  [exchange(): lax.all_to_all(blocks, 'ctx', split_axis=0, concat_axis=0, tiled=True)]
    all_to_all x2 -> x3, starting transfers between devices: 9.21 us -> 23.4 us  [exchange(): lax.all_to_all(blocks, 'ctx', split_axis=0, concat_axis=0, tiled=True)]
    pallas_call x1 -> x2, Pallas kernels: 2.48 us -> 4.01 us  [there(): pl.pallas_call(functools.partial(pack_kernel, heads), out_shape=jax.Shape...]
  transfers between devices with their start and end apart: 2 -> 3, of which waited for: 2 -> 3; matrix products, arithmetic and copies ran while one was open for 1% -> 1% of each run, Pallas kernels for 1% -> 3%
where the time goes in v5:
time: 100 us; the launch traced here: 99.5 us
  blocking collectives  32.7 us (33%)
  waiting for transfers between devices  30.8 us (31%)
  starting transfers between devices  23.4 us (23%)
  Pallas kernels  10.3 us (10%)
    all_to_all x3, waiting for transfers between devices, exchange(): lax.all_to_all(blocks, 'ctx', split_axis=0, concat_axis=0, tiled=True)  30.8 us
    all_to_all x3, starting transfers between devices, exchange(): lax.all_to_all(blocks, 'ctx', split_axis=0, concat_axis=0, tiled=True)  23.4 us
    all_to_all x1, blocking collectives, exchange(): lax.all_to_all(blocks, 'ctx', split_axis=0, concat_axis=0, tiled=True)  16.7 us
    all_gather x1, blocking collectives, on_device(): all_terms = lax.all_gather(own_terms, 'dp')  16 us
    pallas_call x2, Pallas kernels, there(): pl.pallas_call(functools.partial(work_kernel, heads, before), out_shape=o...  4.41 us
    pallas_call x2, Pallas kernels, there(): pl.pallas_call(functools.partial(pack_kernel, heads), out_shape=jax.Shape...  4.01 us
  transfers between devices with their start and end apart: 3, of which 3 were waited for; matrix products, arithmetic and copies ran while one was open for 1% of the time, Pallas kernels for 3%

profile of v5, /device:TPU:1, one launch (start us, length us, event | category | flops | bytes accessed | tf_op | source)
XLA Modules:
  0.0 99.5 jit_solution(8368489776383862727)
XLA Ops:
  0.6 58.5 %conditional.1 = ((bf16[32,7,8,128]{3,2,1,0:T(8,128)(2,1)S(1)}, bf16[32,12,8,128]{3,2,1,0:T(8,128)(2,1)})) conditional(s32[]{:T(128)} %convert_element_type.21, (s32[1,16]{1,0:T(1,128)}, bf16[16,8,1536]{2,1,0:T(8,128)(2,1)}, bf16[16,8,1536]{2,1,0:T(8,128)(2,1)}, bf16[16,8,1536]{2,1,0:T(8,128)(2,1)}, bf16[16,8,1536]{2,1,0:T(8,128)(2,1)}, ...), branch_computations={%region_0.2_spmd, %region_2.4_spmd} | conditional | flops 1006633024 | bytes 24777480 | solution.py:328
  0.7 0.0 copy-start
  0.7 0.0 copy-start.1
  0.7 0.0 copy-start.2
  0.7 0.0 copy-start.4
  0.7 2.0 %pack.3 = bf16[32,8,8,128]{3,2,1,0:T(8,128)(2,1)} custom-call(s32[1,16]{1,0:T(1,128)} %get-tuple-element.29.image_hbm, bf16[16,8,1536]{2,1,0:T(8,128)(2,1)} %get-tuple-element.25.refs_0_, bf16[16,8,1536]{2,1,0:T(8,128)(2,1)} %get-tuple-element.26.refs_1_, bf16[16,8,1536]{2,1,0:T(8,128)(2,1)} %get-tuple-element.27.refs_2_, ...), custom_call_target="tpu_custom_call" | custom-call | bytes 4194304 | tf_op jit(solution)/shard_map/cond/branch_0_fun/pack/pallas_call | solution.py:254
  2.7 13.7 %all-to-all-start = ((bf16[32,8,8,128]{3,2,1,0:T(8,128)(2,1)}), bf16[32,8,8,128]{3,2,1,0:T(8,128)(2,1)S(1)}, u32[]{:S(2)}, u32[]{:S(2)}) async-start(bf16[32,8,8,128]{3,2,1,0:T(8,128)(2,1)} %pack.3), calls=%async_computation | async-start | bytes 1048576 | tf_op jit(solution)/shard_map/cond/branch_0_fun/all_to_all | solution.py:236
  16.4 0.0 copy-done
  16.5 0.0 copy-done.1
  16.5 0.0 copy-done.2
  16.5 0.0 copy-done.4
  16.5 2.0 %pack.4 = bf16[32,16,8,128]{3,2,1,0:T(8,128)(2,1)} custom-call(s32[1,16]{1,0:T(1,128)S(1)} %copy-done.4, bf16[16,8,1536]{2,1,0:T(8,128)(2,1)S(1)} %copy-done, bf16[16,8,1536]{2,1,0:T(8,128)(2,1)S(1)} %copy-done.1, bf16[16,8,1536]{2,1,0:T(8,128)(2,1)S(1)} %copy-done.2, bf16[16,8,1536]{2,1,0:T(8,128)(2,1)} %get-tuple-element.28.refs_3_), custom_call_target="tpu_custom_call" | custom-call | bytes 8388608 | tf_op jit(solution)/shard_map/cond/branch_0_fun/pack/pallas_call | solution.py:254
  18.5 0.0 copy-start.6
  18.5 13.9 %all-to-all-done.blocks_ref = bf16[32,8,8,128]{3,2,1,0:T(8,128)(2,1)S(1)} async-done(((bf16[32,8,8,128]{3,2,1,0:T(8,128)(2,1)}), bf16[32,8,8,128]{3,2,1,0:T(8,128)(2,1)S(1)}, u32[]{:S(2)}, u32[]{:S(2)}) %all-to-all-start) | async-done | bytes 524320 | tf_op jit(solution)/shard_map/cond/branch_0_fun/all_to_all | solution.py:236
  32.4 5.8 %all-to-all-start.1 = ((bf16[32,16,8,128]{3,2,1,0:T(8,128)(2,1)}), bf16[32,16,8,128]{3,2,1,0:T(8,128)(2,1)S(1)}, u32[]{:S(2)}, u32[]{:S(2)}) async-start(bf16[32,16,8,128]{3,2,1,0:T(8,128)(2,1)} %pack.4), calls=%async_computation.1 | async-start | bytes 2097152 | tf_op jit(solution)/shard_map/cond/branch_0_fun/all_to_all | solution.py:236
  38.2 0.7 fusion
  39.6 0.0 copy-done.6
  39.6 1.5 %work.3 = (bf16[32,6,8,128]{3,2,1,0:T(8,128)(2,1)S(1)}, f32[2,128]{1,0:T(2,128)S(1)}) custom-call(s32[1]{0:T(128)S(6)} %convert_element_type.16.long_ref, f32[2,128]{1,0:T(2,128)S(1)} %copy-done.6, bf16[32,8,8,128]{3,2,1,0:T(8,128)(2,1)S(1)} %all-to-all-done.blocks_ref), custom_call_target="tpu_custom_call" | custom-call | flops 335544320 | bytes 917504 | tf_op jit(solution)/shard_map/cond/branch_0_fun/work/pallas_call | solution.py:306
  41.1 15.1 %all-to-all-done.1.blocks_ref = bf16[32,16,8,128]{3,2,1,0:T(8,128)(2,1)S(1)} async-done(((bf16[32,16,8,128]{3,2,1,0:T(8,128)(2,1)}), bf16[32,16,8,128]{3,2,1,0:T(8,128)(2,1)S(1)}, u32[]{:S(2)}, u32[]{:S(2)}) %all-to-all-start.1) | async-done | bytes 1048608 | tf_op jit(solution)/shard_map/cond/branch_0_fun/all_to_all | solution.py:236
  56.2 3.0 %work.4 = (bf16[32,7,8,128]{3,2,1,0:T(8,128)(2,1)S(1)}, bf16[32,12,8,128]{3,2,1,0:T(8,128)(2,1)}) custom-call(s32[1]{0:T(128)S(6)} %convert_element_type.16.long_ref, f32[2,128]{1,0:T(2,128)S(1)} %copy-done.6, bf16[32,16,8,128]{3,2,1,0:T(8,128)(2,1)S(1)} %all-to-all-done.1.blocks_ref, bf16[32,6,8,128]{3,2,1,0:T(8,128)(2,1)S(1)} %get-tuple-element.34.refs_0_, ...), custom_call_target="tpu_custom_call" | custom-call | flops 671088640 | bytes 1835008 | tf_op jit(solution)/shard_map/cond/branch_0_fun/work/pallas_call | solution.py:306
  59.2 0.0 copy-start.3
  59.2 16.7 %all_to_all.22.refs_0_ = bf16[32,7,8,128]{3,2,1,0:T(8,128)(2,1)S(1)} all-to-all(bf16[32,7,8,128]{3,2,1,0:T(8,128)(2,1)S(1)} %get-tuple-element.56), channel_id=1, replica_groups=mesh['dp'=16,'ctx'=32] {'ctx'}, dimensions={0} | all-to-all | bytes 917504 | tf_op jit(solution)/shard_map/all_to_all | solution.py:236
  75.9 3.9 %all-to-all-start.4 = ((bf16[32,12,8,128]{3,2,1,0:T(8,128)(2,1)}), bf16[32,12,8,128]{3,2,1,0:T(8,128)(2,1)S(1)}, u32[]{:S(2)}, u32[]{:S(2)}) async-start(bf16[32,12,8,128]{3,2,1,0:T(8,128)(2,1)} %get-tuple-element.59), calls=%async_computation.4 | async-start | bytes 1572864 | tf_op jit(solution)/shard_map/all_to_all | solution.py:236
  79.9 16.0 %all-gather.1.terms_ref = f32[16,2,128]{2,1,0:T(2,128)S(1)} all-gather(f32[1,2,128]{2,1,0:T(2,128)S(1)} %bitcast.20), channel_id=2, replica_groups=mesh['dp'=16,'ctx'=32] {'dp'}, dimensions={0}, use_global_device_ids=true | all-gather | bytes 17408 | tf_op jit(solution)/shard_map/all_gather | solution.py:342
  95.9 1.7 %all-to-all-done.4.refs_1_ = bf16[32,12,8,128]{3,2,1,0:T(8,128)(2,1)S(1)} async-done(((bf16[32,12,8,128]{3,2,1,0:T(8,128)(2,1)}), bf16[32,12,8,128]{3,2,1,0:T(8,128)(2,1)S(1)}, u32[]{:S(2)}, u32[]{:S(2)}) %all-to-all-start.4) | async-done | bytes 786464 | tf_op jit(solution)/shard_map/all_to_all | solution.py:236
  97.6 0.0 copy-done.3
  97.6 1.8 %unpack.1 = (bf16[16,8,1536]{2,1,0:T(8,128)(2,1)}, bf16[16,8,1536]{2,1,0:T(8,128)(2,1)}, bf16[16,8,1536]{2,1,0:T(8,128)(2,1)}, f32[2,128]{1,0:T(2,128)}) custom-call(s32[1,16]{1,0:T(1,128)S(1)} %copy-done.3, f32[16,2,128]{2,1,0:T(2,128)S(1)} %all-gather.1.terms_ref, bf16[32,7,8,128]{3,2,1,0:T(8,128)(2,1)S(1)} %all_to_all.22.refs_0_, ...), custom_call_target="tpu_custom_call" | custom-call | tf_op jit(solution)/shard_map/unpack/pallas_call | solution.py:344
  (3 shorter events, 0.1 us)
Async XLA Ops:
  0.7 15.8 %copy-start = (bf16[16,8,1536]{2,1,0:T(8,128)(2,1)S(1)}, bf16[16,8,1536]{2,1,0:T(8,128)(2,1)}, u32[]{:S(2)}) copy-start(bf16[16,8,1536]{2,1,0:T(8,128)(2,1)} %get-tuple-element.25.refs_0_) | copy-start | bytes 1179652 | tf_op jit(solution)/shard_map/cond
  0.7 15.8 %copy-start.1 = (bf16[16,8,1536]{2,1,0:T(8,128)(2,1)S(1)}, bf16[16,8,1536]{2,1,0:T(8,128)(2,1)}, u32[]{:S(2)}) copy-start(bf16[16,8,1536]{2,1,0:T(8,128)(2,1)} %get-tuple-element.26.refs_1_) | copy-start | bytes 1179652 | tf_op jit(solution)/shard_map/cond
  0.7 15.8 %copy-start.2 = (bf16[16,8,1536]{2,1,0:T(8,128)(2,1)S(1)}, bf16[16,8,1536]{2,1,0:T(8,128)(2,1)}, u32[]{:S(2)}) copy-start(bf16[16,8,1536]{2,1,0:T(8,128)(2,1)} %get-tuple-element.27.refs_2_) | copy-start | bytes 1179652 | tf_op jit(solution)/shard_map/cond
  0.7 15.8 %copy-start.4 = (s32[1,16]{1,0:T(1,128)S(1)}, s32[1,16]{1,0:T(1,128)}, u32[]{:S(2)}) copy-start(s32[1,16]{1,0:T(1,128)} %get-tuple-element.29.image_hbm) | copy-start | bytes 196 | tf_op jit(solution)/shard_map/cond
  2.7 29.7 %all-to-all-start = ((bf16[32,8,8,128]{3,2,1,0:T(8,128)(2,1)}), bf16[32,8,8,128]{3,2,1,0:T(8,128)(2,1)S(1)}, u32[]{:S(2)}, u32[]{:S(2)}) async-start(bf16[32,8,8,128]{3,2,1,0:T(8,128)(2,1)} %pack.3), calls=%async_computation | async-start | bytes 1048576 | tf_op jit(solution)/shard_map/cond/branch_0_fun/all_to_all | solution.py:236
  18.5 21.1 %copy-start.6 = (f32[2,128]{1,0:T(2,128)S(1)}, f32[2,128]{1,0:T(2,128)}, u32[]{:S(2)}) copy-start(f32[2,128]{1,0:T(2,128)} %get-tuple-element.30.gains_ref) | copy-start | bytes 3076 | tf_op jit(solution)/shard_map/cond
  32.4 23.7 %all-to-all-start.1 = ((bf16[32,16,8,128]{3,2,1,0:T(8,128)(2,1)}), bf16[32,16,8,128]{3,2,1,0:T(8,128)(2,1)S(1)}, u32[]{:S(2)}, u32[]{:S(2)}) async-start(bf16[32,16,8,128]{3,2,1,0:T(8,128)(2,1)} %pack.4), calls=%async_computation.1 | async-start | bytes 2097152 | tf_op jit(solution)/shard_map/cond/branch_0_fun/all_to_all | solution.py:236
  59.2 38.5 %copy-start.3 = (s32[1,16]{1,0:T(1,128)S(1)}, s32[1,16]{1,0:T(1,128)}, u32[]{:S(2)}) copy-start(s32[1,16]{1,0:T(1,128)} %image_ref.1) | copy-start | bytes 196
  75.9 21.8 %all-to-all-start.4 = ((bf16[32,12,8,128]{3,2,1,0:T(8,128)(2,1)}), bf16[32,12,8,128]{3,2,1,0:T(8,128)(2,1)S(1)}, u32[]{:S(2)}, u32[]{:S(2)}) async-start(bf16[32,12,8,128]{3,2,1,0:T(8,128)(2,1)} %get-tuple-element.59), calls=%async_computation.4 | async-start | bytes 1572864 | tf_op jit(solution)/shard_map/all_to_all | solution.py:236

commit v6 on v5

--- a/solution.py
+++ b/solution.py
@@ -15,6 +15,7 @@
 SLOTS = 2
 PIECE_ROWS = 8
 HEAD_DIM = 128
+ALONG_X = 4
 
 PLANS = (((0, 1, 2),), ((0,), (1, 2)))
 BACK = ((2,), (0, 1))
@@ -233,7 +234,11 @@
 
 
 def exchange(blocks):
-    return lax.all_to_all(blocks, "ctx", split_axis=0, concat_axis=0, tiled=True)
+    shards = lax.axis_size("ctx")
+    order = [first + z * ALONG_X for first in range(ALONG_X) for z in range(shards // ALONG_X)]
+    return lax.all_to_all(
+        blocks, "ctx", split_axis=0, concat_axis=0, axis_index_groups=[order], tiled=True
+    )
 
 
 def block_shape(shards, pairs, extra=0):
@@ -243,7 +248,8 @@
 def there(chunks, queries, keys, values, out_grad, norm_gains, tile_image):
     bf16, f32 = jnp.bfloat16, jnp.float32
     shards = lax.axis_size("ctx")
-    place = lax.axis_index("ctx").astype(jnp.int32).reshape(1)
+    own = lax.axis_index("ctx").astype(jnp.int32).reshape(1)
+    place = own % ALONG_X * (shards // ALONG_X) + own // ALONG_X
     sources = (queries, keys, values, out_grad)
     tile_count = queries.shape[0]
     packed = []

time: 100 us -> 99.5 us (level)
  waiting for transfers between devices: 30.8 us -> 25.7 us
  starting transfers between devices: 23.4 us -> 28 us
    all_to_all x3, waiting for transfers between devices: 30.8 us -> 25.7 us  [exchange(): lax.all_to_all(blocks, 'ctx', split_axis=0, concat_axis=0, axis_index_gro...]
    all_to_all x3, starting transfers between devices: 23.4 us -> 28 us  [exchange(): lax.all_to_all(blocks, 'ctx', split_axis=0, concat_axis=0, axis_index_gro...]
  transfers between devices with their start and end apart: 3 -> 3, of which waited for: 3 -> 2; matrix products, arithmetic and copies ran while one was open for 1% -> 1% of each run, Pallas kernels for 3% -> 3%
where the time goes in v6:
time: 99.5 us; the launch traced here: 99 us
  blocking collectives  32.6 us (33%)
  starting transfers between devices  28 us (28%)
  waiting for transfers between devices  25.7 us (26%)
  Pallas kernels  10.3 us (10%)
    all_to_all x3, starting transfers between devices, exchange(): lax.all_to_all(blocks, 'ctx', split_axis=0, concat_axis=0, axis_index_gro...  28 us
    all_to_all x3, waiting for transfers between devices, exchange(): lax.all_to_all(blocks, 'ctx', split_axis=0, concat_axis=0, axis_index_gro...  25.7 us
    all_to_all x1, blocking collectives, exchange(): lax.all_to_all(blocks, 'ctx', split_axis=0, concat_axis=0, axis_index_gro...  16.6 us
    all_gather x1, blocking collectives, on_device(): all_terms = lax.all_gather(own_terms, 'dp')  16 us
    pallas_call x2, Pallas kernels, there(): pl.pallas_call(functools.partial(work_kernel, heads, before), out_shape=o...  4.41 us
    pallas_call x2, Pallas kernels, there(): pl.pallas_call(functools.partial(pack_kernel, heads), out_shape=jax.Shape...  4.01 us
  transfers between devices with their start and end apart: 3, of which 2 were waited for; matrix products, arithmetic and copies ran while one was open for 1% of the time, Pallas kernels for 3%

profile of v6, /device:TPU:1, one launch (start us, length us, event | category | flops | bytes accessed | tf_op | source)
XLA Modules:
  0.0 99.0 jit_solution(8318402993391982593)
XLA Ops:
  0.6 58.4 %conditional.1 = ((bf16[32,7,8,128]{3,2,1,0:T(8,128)(2,1)S(1)}, bf16[32,12,8,128]{3,2,1,0:T(8,128)(2,1)})) conditional(s32[]{:T(128)} %convert_element_type.21, (s32[1,16]{1,0:T(1,128)}, bf16[16,8,1536]{2,1,0:T(8,128)(2,1)}, bf16[16,8,1536]{2,1,0:T(8,128)(2,1)}, bf16[16,8,1536]{2,1,0:T(8,128)(2,1)}, bf16[16,8,1536]{2,1,0:T(8,128)(2,1)}, ...), branch_computations={%region_0.2_spmd, %region_2.4_spmd} | conditional | flops 1006633088 | bytes 24777692 | solution.py:334
  0.7 0.0 copy-start
  0.7 0.0 copy-start.1
  0.7 0.0 copy-start.2
  0.7 0.0 copy-start.4
  0.7 2.0 %pack.3 = bf16[32,8,8,128]{3,2,1,0:T(8,128)(2,1)} custom-call(s32[1,16]{1,0:T(1,128)} %get-tuple-element.29.image_hbm, bf16[16,8,1536]{2,1,0:T(8,128)(2,1)} %get-tuple-element.25.refs_0_, bf16[16,8,1536]{2,1,0:T(8,128)(2,1)} %get-tuple-element.26.refs_1_, bf16[16,8,1536]{2,1,0:T(8,128)(2,1)} %get-tuple-element.27.refs_2_, ...), custom_call_target="tpu_custom_call" | custom-call | bytes 4194304 | tf_op jit(solution)/shard_map/cond/branch_0_fun/pack/pallas_call | solution.py:260
  2.7 13.7 %all-to-all-start = ((bf16[32,8,8,128]{3,2,1,0:T(8,128)(2,1)}), bf16[32,8,8,128]{3,2,1,0:T(8,128)(2,1)S(1)}, u32[]{:S(2)}, u32[]{:S(2)}) async-start(bf16[32,8,8,128]{3,2,1,0:T(8,128)(2,1)} %pack.3), calls=%async_computation | async-start | bytes 1048576 | tf_op jit(solution)/shard_map/cond/branch_0_fun/all_to_all | solution.py:239
  16.4 0.0 copy-done
  16.5 0.0 copy-done.1
  16.5 0.0 copy-done.2
  16.5 0.0 copy-done.4
  16.5 2.0 %pack.4 = bf16[32,16,8,128]{3,2,1,0:T(8,128)(2,1)} custom-call(s32[1,16]{1,0:T(1,128)S(1)} %copy-done.4, bf16[16,8,1536]{2,1,0:T(8,128)(2,1)S(1)} %copy-done, bf16[16,8,1536]{2,1,0:T(8,128)(2,1)S(1)} %copy-done.1, bf16[16,8,1536]{2,1,0:T(8,128)(2,1)S(1)} %copy-done.2, bf16[16,8,1536]{2,1,0:T(8,128)(2,1)} %get-tuple-element.28.refs_3_), custom_call_target="tpu_custom_call" | custom-call | bytes 8388608 | tf_op jit(solution)/shard_map/cond/branch_0_fun/pack/pallas_call | solution.py:260
  18.5 0.0 copy-start.6
  18.5 11.9 %all-to-all-done.blocks_ref = bf16[32,8,8,128]{3,2,1,0:T(8,128)(2,1)S(1)} async-done(((bf16[32,8,8,128]{3,2,1,0:T(8,128)(2,1)}), bf16[32,8,8,128]{3,2,1,0:T(8,128)(2,1)S(1)}, u32[]{:S(2)}, u32[]{:S(2)}) %all-to-all-start) | async-done | bytes 524320 | tf_op jit(solution)/shard_map/cond/branch_0_fun/all_to_all | solution.py:239
  30.4 9.0 %all-to-all-start.1 = ((bf16[32,16,8,128]{3,2,1,0:T(8,128)(2,1)}), bf16[32,16,8,128]{3,2,1,0:T(8,128)(2,1)S(1)}, u32[]{:S(2)}, u32[]{:S(2)}) async-start(bf16[32,16,8,128]{3,2,1,0:T(8,128)(2,1)} %pack.4), calls=%async_computation.1 | async-start | bytes 2097152 | tf_op jit(solution)/shard_map/cond/branch_0_fun/all_to_all | solution.py:239
  39.5 0.7 fusion
  40.8 0.0 copy-done.6
  40.8 1.4 %work.3 = (bf16[32,6,8,128]{3,2,1,0:T(8,128)(2,1)S(1)}, f32[2,128]{1,0:T(2,128)S(1)}) custom-call(s32[1]{0:T(128)S(6)} %convert_element_type.16.long_ref, f32[2,128]{1,0:T(2,128)S(1)} %copy-done.6, bf16[32,8,8,128]{3,2,1,0:T(8,128)(2,1)S(1)} %all-to-all-done.blocks_ref), custom_call_target="tpu_custom_call" | custom-call | flops 335544320 | bytes 917504 | tf_op jit(solution)/shard_map/cond/branch_0_fun/work/pallas_call | solution.py:312
  42.3 13.8 %all-to-all-done.1.blocks_ref = bf16[32,16,8,128]{3,2,1,0:T(8,128)(2,1)S(1)} async-done(((bf16[32,16,8,128]{3,2,1,0:T(8,128)(2,1)}), bf16[32,16,8,128]{3,2,1,0:T(8,128)(2,1)S(1)}, u32[]{:S(2)}, u32[]{:S(2)}) %all-to-all-start.1) | async-done | bytes 1048608 | tf_op jit(solution)/shard_map/cond/branch_0_fun/all_to_all | solution.py:239
  56.1 3.0 %work.4 = (bf16[32,7,8,128]{3,2,1,0:T(8,128)(2,1)S(1)}, bf16[32,12,8,128]{3,2,1,0:T(8,128)(2,1)}) custom-call(s32[1]{0:T(128)S(6)} %convert_element_type.16.long_ref, f32[2,128]{1,0:T(2,128)S(1)} %copy-done.6, bf16[32,16,8,128]{3,2,1,0:T(8,128)(2,1)S(1)} %all-to-all-done.1.blocks_ref, bf16[32,6,8,128]{3,2,1,0:T(8,128)(2,1)S(1)} %get-tuple-element.34.refs_0_, ...), custom_call_target="tpu_custom_call" | custom-call | flops 671088640 | bytes 1835008 | tf_op jit(solution)/shard_map/cond/branch_0_fun/work/pallas_call | solution.py:312
  59.1 0.0 copy-start.3
  59.1 16.6 %all_to_all.22.refs_0_ = bf16[32,7,8,128]{3,2,1,0:T(8,128)(2,1)S(1)} all-to-all(bf16[32,7,8,128]{3,2,1,0:T(8,128)(2,1)S(1)} %get-tuple-element.56), channel_id=1, replica_groups={{0,4,8,12,16,20,24,28,1,5,9,13,17,21,25,29,2,6,10,14,18,22,26,30,3,7,11..., dimensions={0} | all-to-all | bytes 917504 | tf_op jit(solution)/shard_map/all_to_all | solution.py:239
  75.7 5.3 %all-to-all-start.4 = ((bf16[32,12,8,128]{3,2,1,0:T(8,128)(2,1)}), bf16[32,12,8,128]{3,2,1,0:T(8,128)(2,1)S(1)}, u32[]{:S(2)}, u32[]{:S(2)}) async-start(bf16[32,12,8,128]{3,2,1,0:T(8,128)(2,1)} %get-tuple-element.59), calls=%async_computation.4 | async-start | bytes 1572864 | tf_op jit(solution)/shard_map/all_to_all | solution.py:239
  81.1 16.0 %all-gather.1.terms_ref = f32[16,2,128]{2,1,0:T(2,128)S(1)} all-gather(f32[1,2,128]{2,1,0:T(2,128)S(1)} %bitcast.20), channel_id=2, replica_groups=mesh['dp'=16,'ctx'=32] {'dp'}, dimensions={0}, use_global_device_ids=true | all-gather | bytes 17408 | tf_op jit(solution)/shard_map/all_gather | solution.py:348
  97.1 0.0 all-to-all-done.4.refs_1_
  97.1 0.0 copy-done.3
  97.1 1.8 %unpack.1 = (bf16[16,8,1536]{2,1,0:T(8,128)(2,1)}, bf16[16,8,1536]{2,1,0:T(8,128)(2,1)}, bf16[16,8,1536]{2,1,0:T(8,128)(2,1)}, f32[2,128]{1,0:T(2,128)}) custom-call(s32[1,16]{1,0:T(1,128)S(1)} %copy-done.3, f32[16,2,128]{2,1,0:T(2,128)S(1)} %all-gather.1.terms_ref, bf16[32,7,8,128]{3,2,1,0:T(8,128)(2,1)S(1)} %all_to_all.22.refs_0_, ...), custom_call_target="tpu_custom_call" | custom-call | tf_op jit(solution)/shard_map/unpack/pallas_call | solution.py:350
  (3 shorter events, 0.1 us)
Async XLA Ops:
  0.7 15.8 %copy-start = (bf16[16,8,1536]{2,1,0:T(8,128)(2,1)S(1)}, bf16[16,8,1536]{2,1,0:T(8,128)(2,1)}, u32[]{:S(2)}) copy-start(bf16[16,8,1536]{2,1,0:T(8,128)(2,1)} %get-tuple-element.25.refs_0_) | copy-start | bytes 1179652 | tf_op jit(solution)/shard_map/cond
  0.7 15.8 %copy-start.1 = (bf16[16,8,1536]{2,1,0:T(8,128)(2,1)S(1)}, bf16[16,8,1536]{2,1,0:T(8,128)(2,1)}, u32[]{:S(2)}) copy-start(bf16[16,8,1536]{2,1,0:T(8,128)(2,1)} %get-tuple-element.26.refs_1_) | copy-start | bytes 1179652 | tf_op jit(solution)/shard_map/cond
  0.7 15.8 %copy-start.2 = (bf16[16,8,1536]{2,1,0:T(8,128)(2,1)S(1)}, bf16[16,8,1536]{2,1,0:T(8,128)(2,1)}, u32[]{:S(2)}) copy-start(bf16[16,8,1536]{2,1,0:T(8,128)(2,1)} %get-tuple-element.27.refs_2_) | copy-start | bytes 1179652 | tf_op jit(solution)/shard_map/cond
  0.7 15.8 %copy-start.4 = (s32[1,16]{1,0:T(1,128)S(1)}, s32[1,16]{1,0:T(1,128)}, u32[]{:S(2)}) copy-start(s32[1,16]{1,0:T(1,128)} %get-tuple-element.29.image_hbm) | copy-start | bytes 196 | tf_op jit(solution)/shard_map/cond
  2.7 27.7 %all-to-all-start = ((bf16[32,8,8,128]{3,2,1,0:T(8,128)(2,1)}), bf16[32,8,8,128]{3,2,1,0:T(8,128)(2,1)S(1)}, u32[]{:S(2)}, u32[]{:S(2)}) async-start(bf16[32,8,8,128]{3,2,1,0:T(8,128)(2,1)} %pack.3), calls=%async_computation | async-start | bytes 1048576 | tf_op jit(solution)/shard_map/cond/branch_0_fun/all_to_all | solution.py:239
  18.5 22.3 %copy-start.6 = (f32[2,128]{1,0:T(2,128)S(1)}, f32[2,128]{1,0:T(2,128)}, u32[]{:S(2)}) copy-start(f32[2,128]{1,0:T(2,128)} %get-tuple-element.30.gains_ref) | copy-start | bytes 3076 | tf_op jit(solution)/shard_map/cond
  30.4 25.7 %all-to-all-start.1 = ((bf16[32,16,8,128]{3,2,1,0:T(8,128)(2,1)}), bf16[32,16,8,128]{3,2,1,0:T(8,128)(2,1)S(1)}, u32[]{:S(2)}, u32[]{:S(2)}) async-start(bf16[32,16,8,128]{3,2,1,0:T(8,128)(2,1)} %pack.4), calls=%async_computation.1 | async-start | bytes 2097152 | tf_op jit(solution)/shard_map/cond/branch_0_fun/all_to_all | solution.py:239
  59.1 38.0 %copy-start.3 = (s32[1,16]{1,0:T(1,128)S(1)}, s32[1,16]{1,0:T(1,128)}, u32[]{:S(2)}) copy-start(s32[1,16]{1,0:T(1,128)} %image_ref.1) | copy-start | bytes 196
  75.7 21.4 %all-to-all-start.4 = ((bf16[32,12,8,128]{3,2,1,0:T(8,128)(2,1)}), bf16[32,12,8,128]{3,2,1,0:T(8,128)(2,1)S(1)}, u32[]{:S(2)}, u32[]{:S(2)}) async-start(bf16[32,12,8,128]{3,2,1,0:T(8,128)(2,1)} %get-tuple-element.59), calls=%async_computation.4 | async-start | bytes 1572864 | tf_op jit(solution)/shard_map/all_to_all | solution.py:239
